TPU v7x, 256 devices: a whole 4x4x8 slice. The times are simulated.
256 devices in a mesh: feat: 32 (over z_lo, x, core), ex: 8 (over z_hi, y).
Axes of the slice: x: 4, y: 4, z: 8 (z_hi: 2, z_lo: 4; z = z_hi * 4 + z_lo), core: 2. Of those that a mesh axis runs over, the one named last changes fastest.
Arguments:
- activations: bfloat16 [8, 128, 4096], P('ex', None, 'feat'), may hold values from -6 to 6
- output_grads: bfloat16 [8, 128, 14336], P('ex', None, 'feat'), may hold values from -0.52734375 to 0.52734375
- counts: int32 [8], P('ex'), may hold values from 1 to 128
- sign_words: int32 [128, 547], replicated, may hold values from 0 to 1073741823
- coord_row: int32 [4096], replicated, may hold values from 0 to 4095
- coord_col: int32 [4096], replicated, may hold values from 0 to 16383
- queries: float32 [1024, 4096], P('feat', 'ex'), may hold values from -6 to 6
Outputs:
- projected: float32 [8, 4096], P('ex')
- scores: float32 [8, 1024], P('ex', 'feat')
Inputs may be any that keep to these rules, and one draw needn't show every extreme that they name: `sign_words`: bits 0 to 29 of each word are signs; columns past 16384 are unused.
All inputs are finite; a program needn't handle non-finite values.
Results may differ from a plain program's by a relative error of at most 0.0003.
Values may be sent and summed in bfloat16 or wider, within the bound.
No kernel may reach another device: no remote copies, remote signals or barrier semaphores. Data moves between devices by JAX's collectives and lax.ppermute only.
A program may use at most 128 MiB of HBM per device.

v0:
```python
import math

import jax
import jax.numpy as jnp
from jax import lax
from jax.sharding import PartitionSpec as P

DIN = 4096
DPAD = 16384
PROJ = 4096


def parity_signs(left_ids, right_ids, bit_count):
    common = jnp.bitwise_and(left_ids, right_ids)
    running = jnp.zeros(common.shape, jnp.int32)
    for position in range(bit_count):
        running = running + jnp.bitwise_and(jnp.right_shift(common, position), 1)
    return (1 - 2 * jnp.bitwise_and(running, 1)).astype(jnp.float32)


def sylvester(order_size):
    indices = jnp.arange(order_size, dtype=jnp.int32)
    return parity_signs(indices[:, None], indices[None, :], order_size.bit_length() - 1)


def walsh_axis(field, dim_at):
    length = field.shape[dim_at]
    factors = []
    remain = length
    while remain > 1:
        factor = min(remain, 128)
        factors.append(factor)
        remain = remain // factor
    leading = field.shape[:dim_at]
    trailing = field.shape[dim_at + 1 :]
    reshaped = field.reshape(leading + tuple(factors) + trailing)
    labels = "abcdefghijklmnopqrstuvw"[: reshaped.ndim]
    for place, factor in enumerate(factors):
        target = dim_at + place
        result_labels = labels[:target] + "z" + labels[target + 1 :]
        reshaped = jnp.einsum(
            labels + "," + labels[target] + "z->" + result_labels,
            reshaped,
            sylvester(factor),
            precision=lax.Precision.HIGHEST,
        )
    return reshaped.reshape(field.shape)


def unpack_signs(sign_words, length):
    shifts = jnp.arange(30, dtype=jnp.int32)
    bit_values = jnp.bitwise_and(jnp.right_shift(sign_words[:, :, None], shifts), 1)
    unpacked = bit_values.reshape(sign_words.shape[0], sign_words.shape[1] * 30)[:, :length]
    return (1 - 2 * unpacked).astype(jnp.bfloat16)


def body(activations, output_grads, counts, sign_words, coord_row, coord_col, queries):
    tokens = activations.shape[1]
    cols_here = output_grads.shape[2]
    feat_index = lax.axis_index("feat")
    live_mask = (jnp.arange(tokens, dtype=jnp.int32)[None, :] < counts[:, None]).astype(
        jnp.bfloat16
    )
    sign_table = unpack_signs(sign_words, DPAD)
    norm_scale = 1.0 / math.sqrt(DIN * DPAD)
    masked_grads = output_grads * live_mask[:, :, None]
    first_col = feat_index * cols_here
    col_table = lax.dynamic_slice_in_dim(sign_table, first_col, cols_here, 1)
    tall_table = jnp.tile(col_table, (DIN // col_table.shape[0], 1))
    outer_block = jnp.einsum(
        "etr,etc->erc",
        lax.all_gather(activations, "feat", axis=2, tiled=True),
        masked_grads,
        preferred_element_type=jnp.float32,
    )
    signed = outer_block * tall_table[None]
    mixed_field = walsh_axis(signed, 1)
    picked = jnp.take(mixed_field, coord_row, axis=1)
    global_cols = first_col + jnp.arange(cols_here, dtype=jnp.int32)
    col_signs = parity_signs(coord_col[:, None], global_cols[None, :], DPAD.bit_length() - 1)
    partial_value = jnp.einsum("ekc,kc->ek", picked, col_signs, precision=lax.Precision.HIGHEST)
    projected = lax.psum(partial_value * norm_scale, "feat")
    rescale = 1.0 / math.sqrt(PROJ)
    full_queries = lax.all_gather(queries, "ex", axis=1, tiled=True)
    scores = jnp.dot(projected, full_queries.T, precision=lax.Precision.HIGHEST) * rescale
    return (projected, scores)


def solution(mesh):
    return jax.shard_map(
        body,
        mesh=mesh,
        in_specs=(
            P("ex", None, "feat"),
            P("ex", None, "feat"),
            P("ex"),
            P(),
            P(),
            P(),
            P("feat", "ex"),
        ),
        out_specs=(P("ex", None), P("ex", "feat")),
        check_vma=False,
    )
```

profile of v0, /device:TPU:8, one launch (start us, length us, event | category | flops | bytes accessed | tf_op | source)
XLA Modules:
  0.0 325.0 jit_solution(7652090999071195045)
XLA Ops:
  7.2 0.0 copy-start.2
  7.2 0.0 all-gather.2.cloned.1.call-start
  7.2 0.7 all-gather.2.cloned.1.call-update
  7.9 12.9 %fusion.29 = f32[4096,448]{0,1:T(8,128)} fusion(s32[448]{0:T(512)S(1)} %iota_add_fusion, s32[4096]{0:T(1024)} %param.12), kind=kLoop, calls=%fused_computation.45 | loop fusion | flops 84410368 | bytes 7358208 | tf_op jit(solution)/shard_map/convert_element_type | solution.py:18
  20.9 0.2 shift_right_arithmetic.207
  21.1 0.0 copy-start.3
  21.1 0.0 copy-done.2
  21.1 4.0 %shift_right_arithmetic.204 = s32[128,547,30]{0,2,1:T(8,128)} broadcast(s32[128,547]{0,1:T(8,128)S(1)} %copy-done.2), dimensions={0,1} | broadcast | bytes 8681984 | tf_op jit(solution)/shard_map/shift_right_arithmetic | solution.py:52
  25.2 9.4 %shift_right_arithmetic.205 = s32[128,16410]{0,1:T(8,128)} reshape(s32[128,547,30]{0,2,1:T(8,128)} %shift_right_arithmetic.204) | data formatting | bytes 16803840 | tf_op jit(solution)/shard_map/shift_right_arithmetic | solution.py:52
  34.5 0.0 copy-done.3
  34.5 5.8 %slice.6 = s32[128,16384]{0,1:T(8,128)} slice(s32[128,16410]{0,1:T(8,128)} %shift_right_arithmetic.205), slice={[0:128], [0:16384]} | slice | bytes 16777216 | tf_op jit(solution)/shard_map/slice | solution.py:53
  41.0 0.0 slice-start
  41.0 0.0 copy-start.6
  41.0 0.0 copy-start.4
  41.0 9.0 %copy.17 = f32[4096,448]{1,0:T(8,128)} copy(f32[4096,448]{0,1:T(8,128)} %fusion.29) | data formatting | bytes 14680064
  50.0 0.0 copy-start.1
  50.0 0.0 slice-done
  50.0 0.1 dynamic-slice
  50.1 0.0 copy-done.6
  50.1 0.0 copy-done.4
  50.1 46.8 %all_gather.7 = f32[32,4096]{1,0:T(8,128)S(1)} all-gather(f32[32,512]{1,0:T(8,128)S(1)} %copy-done.4), channel_id=1, replica_groups=mesh['feat'=32,'ex'=8] {'ex'}, dimensions={1}, use_global_device_ids=true | all-gather | bytes 589824 | tf_op jit(solution)/shard_map/all_gather | solution.py:84
  96.9 1.1 fusion.38
  98.0 0.0 all-gather.2.cloned.1.call-done
  98.0 0.0 copy-start
  98.1 0.5 tile.2
  98.5 0.0 copy-done.1
  98.5 0.7 copy-done
  99.3 7.6 %bitcast_multiply_fusion = f32[4096,448]{0,1:T(8,128)} fusion(f32[56,8,32,128]{3,2,1,0:T(8,128)S(1)} %bitcast.46, bf16[1,128,4096]{2,1,0:T(8,128)(2,1)S(1)} %copy-done, bf16[1,128,448]{1,2,0:T(8,128)(2,1)S(1)} %copy-done.1, bf16[128]{0:T(256)(128)(2,1)S(1)} %compare_convert_fusion), kind=kOutput, calls=%fused_computation.47 | convolution fusion | flops 471654400 | bytes 15843584 | tf_op jit(solution)/shard_map/etr,etc->erc/dot_general | solution.py:70
  106.8 8.9 %copy.11 = f32[4096,448]{1,0:T(8,128)} copy(f32[4096,448]{0,1:T(8,128)} %bitcast_multiply_fusion) | data formatting | bytes 14680064 | tf_op jit(solution)/shard_map/mul | solution.py:76
  115.8 10.9 %copy.12 = f32[128,32,448]{0,1,2:T(8,128)} copy(f32[128,32,448]{2,1,0:T(8,128)} %bitcast.47) | data formatting | bytes 14680064 | tf_op jit(solution)/shard_map/reshape.12
  126.6 10.5 %fusion.41 = f32[128,32,448]{0,1,2:T(8,128)S(1)} fusion(f32[128,32,448]{0,1,2:T(8,128)} %copy.12), kind=kOutput, calls=%fused_computation.61 | convolution fusion | flops 2818981888 | bytes 14680064 | tf_op jit(solution)/shard_map/abcd,bz->azcd/dot_general | solution.py:41
  137.2 8.3 %convolution_bitcast_fusion = f32[1,128,32,448]{1,2,3,0:T(8,128)} fusion(f32[128,32,448]{0,1,2:T(8,128)S(1)} %fusion.41), kind=kOutput, calls=%fused_computation.48 | convolution fusion | flops 704662528 | bytes 14680064 | tf_op jit(solution)/shard_map/abcd,cz->abzd/dot_general | solution.py:41
  145.4 10.4 %copy.13 = f32[1,128,32,448]{3,2,1,0:T(8,128)} copy(f32[1,128,32,448]{1,2,3,0:T(8,128)} %convolution_bitcast_fusion) | data formatting | bytes 14680064 | tf_op jit(solution)/shard_map/abcd,cz->abzd/transpose | solution.py:41
  155.9 21.4 %gather_fusion = f32[4096,448]{1,0:T(8,128)} fusion(f32[4096,448]{1,0:T(8,128)} %bitcast.45, s32[4096]{0:T(1024)S(1)} %fusion.101), kind=kCustom, calls=%fused_computation | custom fusion | bytes 14696448 | tf_op jit(solution)/shard_map/jit(_take)/gather | solution.py:78
  177.3 6.7 %multiply_reduce_fusion = f32[4096]{0:T(1024)S(1)} fusion(f32[4096,448]{1,0:T(8,128)} %copy.17, f32[4096,448]{1,0:T(8,128)} %gather_fusion, pred[4096]{0:T(1024)(128)(4,1)S(1)} %compare_and_fusion), kind=kLoop, calls=%fused_computation.15 | loop fusion | flops 5500928 | bytes 14700544 | tf_op jit(solution)/shard_map/ekc,kc->ek/dot_general | solution.py:81
  184.0 133.2 %psum.7 = f32[1,4096]{1,0:T(1,128)S(1)} all-reduce(f32[1,4096]{1,0:T(1,128)S(1)} %bitcast.48), channel_id=1, replica_groups=mesh['feat'=32,'ex'=8] {'feat'}, use_global_device_ids=true, to_apply=%region_0.1 | all-reduce | flops 4096 | bytes 32768 | tf_op jit(solution)/shard_map/psum | solution.py:82
  317.1 0.0 copy-start.5
  317.1 1.0 fusion.32
  318.2 0.0 copy-done.5
  (6 shorter events, 0.0 us)
Async XLA Ops:
  7.2 13.9 %copy-start.2 = (s32[128,547]{0,1:T(8,128)S(1)}, s32[128,547]{0,1:T(8,128)}, u32[]{:S(2)}) copy-start(s32[128,547]{0,1:T(8,128)} %param.10) | copy-start | bytes 840196
  7.2 90.9 %all-gather.2.cloned.1.call-start = ((), (), s32[]{:S(2)}) async-start(), calls=%async_computation | async-start | bytes 1081344 | tf_op jit(solution)/shard_map/all_gather | solution.py:72
  21.1 13.4 %copy-start.3 = (s32[16410]{0:T(1024)}, s32[16410]{0:T(1024)S(1)}, u32[]{:S(2)}) copy-start(s32[16410]{0:T(1024)S(1)} %shift_right_arithmetic.207) | copy-start | bytes 196924
  41.0 9.1 %slice-start = ((s32[16410]{0:T(1024)}), s32[16384]{0:T(1024)S(1)}, s32[]{:S(2)}) async-start(s32[16410]{0:T(1024)} %copy-done.3), calls=%async_computation.1 | async-start | bytes 131072 | tf_op jit(solution)/shard_map/slice | solution.py:53
  41.0 9.1 %copy-start.6 = (s32[4096]{0:T(1024)S(1)}, s32[4096]{0:T(1024)}, u32[]{:S(2)}) copy-start(s32[4096]{0:T(1024)} %param.11) | copy-start | bytes 49156
  41.0 9.2 %copy-start.4 = (f32[32,512]{1,0:T(8,128)S(1)}, f32[32,512]{1,0:T(8,128)}, u32[]{:S(2)}) copy-start(f32[32,512]{1,0:T(8,128)} %param.13) | copy-start | bytes 196612
  50.0 48.5 %copy-start.1 = (bf16[1,128,448]{1,2,0:T(8,128)(2,1)S(1)}, bf16[1,128,448]{1,2,0:T(8,128)(2,1)}, u32[]{:S(2)}) copy-start(bf16[1,128,448]{1,2,0:T(8,128)(2,1)} %param.8) | copy-start | bytes 344068
  98.0 1.2 copy-start
  317.1 1.0 copy-start.5
Sparse Core Ops, SparseCore 0:
  9.8 63.4 all-gather.1
where the time goes:
time: 326 us; the launch traced here: 325 us
  blocking collectives  180 us (55%)
  local copies, waits for them, and re-layouts  81.4 us (25%)
  matrix products  27.4 us (8%)
  other arithmetic  20.7 us (6%)
  between operations  14.8 us (5%)
    psum x1, blocking collectives, body(): projected = lax.psum(partial_value * norm_scale, 'feat')  133 us
    all_gather x1, blocking collectives, body(): full_queries = lax.all_gather(queries, 'ex', axis=1, tiled=True)  46.8 us
    gather x1, local copies, waits for them, and re-layouts, body(): picked = jnp.take(mixed_field, coord_row, axis=1)  21.4 us
    dot_general x2, matrix products, walsh_axis(): jnp.einsum(labels + ',' + labels[target] + 'z->' + result_labels, reshape...  18.8 us
    shift_right_arithmetic x4, local copies, waits for them, and re-layouts, unpack_signs(): jnp.right_shift(sign_words[:, :, None], shifts)  13.6 us
    convert_element_type x1, other arithmetic, parity_signs(): return (1 - 2 * jnp.bitwise_and(running, 1)).astype(jnp.float32)  12.9 us
    another operation x1, local copies, waits for them, and re-layouts  10.9 us
    transpose x1, local copies, waits for them, and re-layouts, walsh_axis(): jnp.einsum(labels + ',' + labels[target] + 'z->' + result_labels, reshape...  10.4 us
  transfers between devices with their start and end apart: 1, of which 0 were waited for; matrix products, arithmetic and copies ran while one was open for 13% of the time, Pallas kernels for 0%

commit v1 on v0

v1 whole, which is shorter than its diff:
```python
import math

import jax
import jax.numpy as jnp
from jax import lax
from jax.experimental import pallas as pl
from jax.experimental.pallas import tpu as pltpu
from jax.sharding import PartitionSpec as P

DIN = 4096
DPAD = 16384
PROJ = 4096
TOK = 128
COLS = 448
RUNS = COLS // 64
GROUPS = 8
BLK = 256
MAXB = 24
HOTS = 32

ROW_STEPS = (16, 8, 6)
COL_STEPS = (1, 2)
SUM_STEPS = (1, 2, 6, 8, 16)
EX_STEPS = (4, 1, 3)

F32 = jnp.float32
BF16 = jnp.bfloat16
I32 = jnp.int32
NT = (((1,), (1,)), ((), ()))


def iota(shape, dim):
    return lax.broadcasted_iota(I32, shape, dim)


def parity(bits):
    bits = bits ^ (bits >> 4)
    bits = bits ^ (bits >> 2)
    bits = bits ^ (bits >> 1)
    return bits & 1


def sign_of(bit):
    return (1 - 2 * bit).astype(F32)


def one_hot(cond):
    return jnp.where(cond, 1.0, 0.0)


def sort_kernel(row_ref, col_ref, sorted_ref, low_ref, high_ref, info_ref, value_ref):
    row = row_ref[...]
    col = col_ref[...]
    block_row = row >> 7
    key = (
        ((block_row >> 4) & 1)
        | (((block_row >> 3) & 1) << 1)
        | ((((block_row >> 1) ^ (block_row >> 2)) & 1) << 2)
    )
    hot = jnp.concatenate([one_hot(key == g) for g in range(GROUPS)], axis=0).astype(BF16)
    upper = one_hot(iota((128, 128), 0) <= iota((128, 128), 1)).astype(BF16)
    within = jnp.dot(hot, upper, preferred_element_type=F32)
    sums = jnp.dot(hot, jnp.ones((128, 128), BF16), preferred_element_type=F32)
    here, there = iota((256, 256), 0), iota((256, 256), 1)
    earlier = one_hot(((here >> 5) == (there >> 5)) & (there < here)).astype(BF16)
    before = jnp.dot(earlier, sums.astype(BF16), preferred_element_type=F32)
    rank = within + before - 1.0
    lane = iota((1, 128), 1)
    base = jnp.zeros((1, 128), I32)
    owner = jnp.zeros((1, 128), I32)
    place = jnp.zeros((32, 128), F32)
    for g in range(GROUPS):
        last = 32 * g + 31
        total = (before[last : last + 1] + sums[last : last + 1]).astype(I32)
        place = place + jnp.where(
            key == g, rank[32 * g : 32 * g + 32] + (base << 8).astype(F32), 0.0
        )
        base = base + ((total + (BLK - 1)) >> 8)
        owner = owner + jnp.where(base <= lane, 1, 0)
    info_ref[...] = jnp.concatenate([owner, base, jnp.zeros((6, 128), I32)], axis=0)
    place = place.astype(I32)
    for i in range(32):
        at = slice(128 * i, 128 * i + 128)
        spot = place[i : i + 1]
        low_ref[:, at] = one_hot(iota((BLK, 128), 0) == (spot & (BLK - 1))).astype(BF16)
        high = one_hot(iota((HOTS, 128), 0) == (spot >> 8))
        high_ref[:, at] = high.astype(BF16)
        r, c = row[i : i + 1], col[i : i + 1]
        fields = (r & 127, r >> 7, c >> 6, c & 63)
        value_ref[:, at] = jnp.concatenate(
            [high * field.astype(F32) for field in fields], axis=0
        ).astype(BF16)
    sorted_ref[...] = lax.dot_general(
        value_ref[...], low_ref[...], NT, preferred_element_type=F32
    ).astype(I32)


def sort_coords(coord_row, coord_col):
    return pl.pallas_call(
        sort_kernel,
        out_shape=(
            jax.ShapeDtypeStruct((4 * HOTS, BLK), I32),
            jax.ShapeDtypeStruct((BLK, PROJ), BF16),
            jax.ShapeDtypeStruct((HOTS, PROJ), BF16),
            jax.ShapeDtypeStruct((8, 128), I32),
        ),
        scratch_shapes=[pltpu.VMEM((4 * HOTS, PROJ), BF16)],
        cost_estimate=pl.CostEstimate(flops=10**9, bytes_accessed=3 * 10**6, transcendentals=0),
        name="sort_coords",
    )(coord_row.reshape(32, 128), coord_col.reshape(32, 128))


def coord_signs_kernel(place_ref, sorted_ref, u_ref, vl_ref, vj_ref):
    feat = place_ref[0]

    def step(b, carry):
        low_row = sorted_ref[pl.ds(b, 1), :]
        block_row = sorted_ref[pl.ds(HOTS + b, 1), :]
        col_high = sorted_ref[pl.ds(2 * HOTS + b, 1), :]
        col_low = sorted_ref[pl.ds(3 * HOTS + b, 1), :]
        u_ref[b] = sign_of(parity(iota((128, BLK), 0) & low_row)).astype(BF16)
        flip = parity(block_row & feat)
        vl_ref[b] = sign_of(parity(iota((64, BLK), 0) & col_low) ^ flip) * (
            1.0 / math.sqrt(DIN * DPAD)
        )
        piece = iota((32, BLK), 0)
        run = RUNS * (feat ^ (piece >> 3)) + (piece & 7)
        vj_ref[b] = sign_of(parity(run & col_high))
        return carry

    lax.fori_loop(0, MAXB, step, 0)


def coord_signs(place, sorted_fields):
    return pl.pallas_call(
        coord_signs_kernel,
        out_shape=(
            jax.ShapeDtypeStruct((MAXB, 128, BLK), BF16),
            jax.ShapeDtypeStruct((MAXB, 64, BLK), F32),
            jax.ShapeDtypeStruct((MAXB, 32, BLK), F32),
        ),
        in_specs=[
            pl.BlockSpec(memory_space=pltpu.SMEM),
            pl.BlockSpec(memory_space=pltpu.VMEM),
        ],
        cost_estimate=pl.CostEstimate(flops=10**9, bytes_accessed=4 * 10**6, transcendentals=0),
        name="coord_signs",
    )(place, sorted_fields)


def table_kernel(place_ref, words_ref, sign_ref):
    feat = place_ref[0]
    words = words_ref[...]
    octets = jnp.concatenate(
        [((words >> (8 * p)) & 255).astype(F32) for p in range(4)], axis=1
    ).astype(BF16)
    first_word = ((4 * COLS * (feat >> 2)) * 34953) >> 20
    for e in range(4):
        col = COLS * (feat ^ e) + iota((COLS, 128), 0)
        word = (col * 34953) >> 20
        bit = col - 30 * word
        target = ((bit >> 3) << 6) + (word - first_word)
        lane = iota((COLS, 128), 1)
        pick = jnp.concatenate(
            [one_hot(lane == target), one_hot(lane + 128 == target)], axis=1
        ).astype(BF16)
        octet = lax.dot_general(pick, octets, NT, preferred_element_type=F32).astype(I32)
        sign_ref[e] = sign_of((octet >> (bit & 7)) & 1)


def sign_table(place, words):
    return pl.pallas_call(
        table_kernel,
        out_shape=jax.ShapeDtypeStruct((4, COLS, 128), F32),
        in_specs=[
            pl.BlockSpec(memory_space=pltpu.SMEM),
            pl.BlockSpec(memory_space=pltpu.VMEM),
        ],
        cost_estimate=pl.CostEstimate(flops=10**9, bytes_accessed=10**6, transcendentals=0),
        name="sign_table",
    )(place, words)


def split(value):
    high = value.astype(BF16)
    return high, (value - high.astype(F32)).astype(BF16)


def main_kernel(
    info_ref, a_ref, g_ref, sign_ref, u_ref, vl_ref, vj_ref, out_ref, mixed_ref, signed_ref
):
    for first in range(0, TOK, 32):
        rows = slice(first, first + 32)
        parts = [a_ref[i, rows, :].astype(F32) for i in range(GROUPS)]
        for bit in (1, 2, 4):
            for i in range(GROUPS):
                if not i & bit:
                    parts[i], parts[i | bit] = (
                        parts[i] + parts[i | bit],
                        parts[i] - parts[i | bit],
                    )
        for i in range(GROUPS):
            high, low = split(parts[i])
            mixed_ref[rows, 128 * i : 128 * i + 128] = high
            mixed_ref[TOK + first : TOK + first + 32, 128 * i : 128 * i + 128] = low
    for e in range(4):
        grads = jnp.concatenate([g_ref[e], g_ref[e]], axis=1)
        signs = sign_ref[e]
        here = slice(COLS * e, COLS * e + COLS)
        for pair in range(GROUPS // 2):
            outer = jnp.dot(
                grads, mixed_ref[:, 256 * pair : 256 * pair + 256], preferred_element_type=F32
            )
            for half in range(2):
                high, low = split(outer[:, 128 * half : 128 * half + 128] * signs)
                signed_ref[2 * pair + half, here, 0:128] = high
                signed_ref[2 * pair + half, here, 128:256] = low
    out_ref[...] = jnp.zeros_like(out_ref)

    def block(b, carry):
        group = info_ref[0, b]
        weights = jnp.concatenate([u_ref[b], u_ref[b]], axis=0)
        total = jnp.zeros((64, BLK), F32)
        for e in range(4):
            here = slice(COLS * e, COLS * e + COLS)
            rows = jnp.dot(signed_ref[group, here, :], weights, preferred_element_type=F32)
            for j in range(RUNS):
                total = total + vj_ref[b, 8 * e + j : 8 * e + j + 1, :] * rows[64 * j : 64 * j + 64]
        out_ref[pl.ds(b, 1), :] = jnp.sum(total * vl_ref[b], axis=0, keepdims=True)
        return carry

    lax.fori_loop(0, info_ref[1, 0], block, 0)


def partial_sums(info, acts, grads, signs, u, vl, vj):
    vmem = pl.BlockSpec(memory_space=pltpu.VMEM)
    return pl.pallas_call(
        main_kernel,
        out_shape=jax.ShapeDtypeStruct((MAXB, BLK), F32),
        in_specs=[pl.BlockSpec(memory_space=pltpu.SMEM)] + [vmem] * 6,
        out_specs=vmem,
        scratch_shapes=[
            pltpu.VMEM((2 * TOK, GROUPS * 128), BF16),
            pltpu.VMEM((GROUPS, 4 * COLS, 256), BF16),
        ],
        cost_estimate=pl.CostEstimate(flops=10**10, bytes_accessed=10**7, transcendentals=0),
        compiler_params=pltpu.CompilerParams(vmem_limit_bytes=40 * 2**20),
        name="partial_sums",
    )(info, acts, grads, signs, u, vl, vj)


def finish_kernel(place_ref, mine_ref, other_ref, low_ref, high_ref, q_ref, proj_ref, score_ref, row_ref):
    ex = place_ref[1]
    total = mine_ref[...] + other_ref[...]
    total = jnp.concatenate([total, jnp.zeros((HOTS - MAXB, BLK), F32)], axis=0)
    high, low = split(total)
    picked = jnp.dot(
        jnp.concatenate([high, low], axis=0), low_ref[...], preferred_element_type=F32
    )
    picked = (picked[:HOTS] + picked[HOTS:]) * high_ref[...].astype(F32)
    proj = jnp.sum(picked, axis=0, keepdims=True)
    proj_ref[...] = proj
    for s in range(8):
        row_ref[s : s + 1, :] = proj[:, 512 * s : 512 * s + 512]
    order = [0]
    for step in EX_STEPS:
        order = order + [d ^ step for d in order]
    acc = jnp.zeros((32, 512), F32)
    for spot, d in enumerate(order):
        acc = acc + q_ref[spot] * row_ref[pl.ds(ex ^ d, 1), :]
    acc = (acc[:, 0:128] + acc[:, 128:256]) + (acc[:, 256:384] + acc[:, 384:512])
    scores = lax.dot_general(
        jnp.ones((8, 128), F32), acc, NT, precision=lax.Precision.HIGHEST, preferred_element_type=F32
    )
    score_ref[...] = scores[0:1] * (1.0 / math.sqrt(PROJ))


def finish(place, mine, other, low, high, queries):
    vmem = pl.BlockSpec(memory_space=pltpu.VMEM)
    return pl.pallas_call(
        finish_kernel,
        out_shape=(
            jax.ShapeDtypeStruct((1, PROJ), F32),
            jax.ShapeDtypeStruct((1, 32), F32),
        ),
        in_specs=[pl.BlockSpec(memory_space=pltpu.SMEM)] + [vmem] * 5,
        out_specs=(vmem, vmem),
        scratch_shapes=[pltpu.VMEM((8, 512), F32)],
        name="finish",
    )(place, mine, other, low, high, queries)


def swap(value, axis, size, step):
    return lax.ppermute(value, axis, [(i, i ^ step) for i in range(size)])


def gather_by(value, axis, size, steps):
    value = value[None]
    for step in steps:
        value = jnp.concatenate([value, swap(value, axis, size, step)], axis=0)
    return value


def body(activations, output_grads, counts, sign_words, coord_row, coord_col, queries):
    feat = lax.axis_index("feat")
    ex = lax.axis_index("ex")
    place = jnp.stack([feat, ex]).astype(I32)
    live = jnp.arange(TOK, dtype=I32)[:, None] < counts[0]
    own_grads = jnp.where(live, output_grads[0], jnp.zeros((), BF16)).T
    acts = gather_by(activations[0], "feat", 32, ROW_STEPS)
    grads = gather_by(own_grads, "feat", 32, COL_STEPS)
    all_queries = gather_by(queries, "ex", 8, EX_STEPS)

    sorted_fields, low, high, info = sort_coords(coord_row, coord_col)
    u, vl, vj = coord_signs(place, sorted_fields)
    window = lax.dynamic_slice(sign_words, (0, (4 * COLS * (feat // 4)) // 30), (128, 64))
    signs = sign_table(place, window)
    total = partial_sums(info, acts, grads, signs, u, vl, vj)
    for step in SUM_STEPS[:-1]:
        total = total + swap(total, "feat", 32, step)
    other = swap(total, "feat", 32, SUM_STEPS[-1])
    return finish(place, total, other, low, high, all_queries)


def solution(mesh):
    return jax.shard_map(
        body,
        mesh=mesh,
        in_specs=(
            P("ex", None, "feat"),
            P("ex", None, "feat"),
            P("ex"),
            P(),
            P(),
            P(),
            P("feat", "ex"),
        ),
        out_specs=(P("ex", None), P("ex", "feat")),
        check_vma=False,
    )
```

time: 326 us -> 74.4 us (0.23)
  blocking collectives: 180 us -> 0 us
  local copies, waits for them, and re-layouts: 81.4 us -> 3.9 us
  matrix products: 27.4 us -> 0 us
  Pallas kernels: 0 us -> 26.4 us
  waiting for transfers between devices: 0.7 us -> 21.4 us
  starting transfers between devices: 0.04 us -> 18.9 us
  other arithmetic: 20.7 us -> 2.54 us
  between operations: 14.8 us -> 1.42 us
    psum x1 -> x0, blocking collectives: 133 us -> none  [body(): projected = lax.psum(partial_value * norm_scale, 'feat')]
    all_gather x1 -> x0, blocking collectives: 46.8 us -> none  [body(): full_queries = lax.all_gather(queries, 'ex', axis=1, tiled=True)]
    dot_general x4 -> x0, matrix products: 27.4 us -> none  [the longest x2 18.8 us: walsh_axis(): jnp.einsum(labels + ',' + labels[target] + 'z->' + result_labels, reshape...]
    pallas_call x0 -> x5, Pallas kernels: none -> 26.4 us  [the longest x1 11.9 us: partial_sums(): pl.pallas_call(main_kernel, out_shape=jax.ShapeDtypeStruct((MAXB, BLK), F...]
    gather x1 -> x0, local copies, waits for them, and re-layouts: 21.4 us -> none  [body(): picked = jnp.take(mixed_field, coord_row, axis=1)]
    ppermute x0 -> x13, waiting for transfers between devices: none -> 21.4 us  [swap(): return lax.ppermute(value, axis, [(i, i ^ step) for i in range(size)])]
    ppermute x0 -> x13, starting transfers between devices: none -> 18.9 us  [swap(): return lax.ppermute(value, axis, [(i, i ^ step) for i in range(size)])]
    convert_element_type x3 -> x0, other arithmetic: 14 us -> none  [the longest x1 12.9 us: parity_signs(): return (1 - 2 * jnp.bitwise_and(running, 1)).astype(jnp.float32)]
  transfers between devices with their start and end apart: 1 -> 13, of which waited for: 0 -> 8; matrix products, arithmetic and copies ran while one was open for 13% -> 4% of each run, Pallas kernels for 0% -> 31%
where the time goes in v1:
time: 74.4 us; the launch traced here: 74.5 us
  Pallas kernels  26.4 us (35%)
  waiting for transfers between devices  21.4 us (29%)
  starting transfers between devices  18.9 us (25%)
  local copies, waits for them, and re-layouts  3.9 us (5%)
  other arithmetic  2.54 us (3%)
  between operations  1.42 us (2%)
    ppermute x13, waiting for transfers between devices, swap(): return lax.ppermute(value, axis, [(i, i ^ step) for i in range(size)])  21.4 us
    ppermute x13, starting transfers between devices, swap(): return lax.ppermute(value, axis, [(i, i ^ step) for i in range(size)])  18.9 us
    pallas_call x1, Pallas kernels, partial_sums(): pl.pallas_call(main_kernel, out_shape=jax.ShapeDtypeStruct((MAXB, BLK), F...  11.9 us
    pallas_call x1, Pallas kernels, coord_signs(): pl.pallas_call(coord_signs_kernel, out_shape=(jax.ShapeDtypeStruct((MAXB,...  5.22 us
    unnamed x21, local copies, waits for them, and re-layouts  3.89 us
    pallas_call x1, Pallas kernels, sort_coords(): pl.pallas_call(sort_kernel, out_shape=(jax.ShapeDtypeStruct((4 * HOTS, BL...  3.72 us
    pallas_call x1, Pallas kernels, finish(): pl.pallas_call(finish_kernel, out_shape=(jax.ShapeDtypeStruct((1, PROJ),...  3.02 us
    pallas_call x1, Pallas kernels, sign_table(): pl.pallas_call(table_kernel, out_shape=jax.ShapeDtypeStruct((4, COLS, 128...  2.53 us
  transfers between devices with their start and end apart: 13, of which 8 were waited for; matrix products, arithmetic and copies ran while one was open for 4% of the time, Pallas kernels for 31%

profile of v1, /device:TPU:8, one launch (start us, length us, event | category | flops | bytes accessed | tf_op | source)
XLA Modules:
  0.0 74.5 jit_solution(2715381076443709676)
XLA Ops:
  0.6 0.0 copy-start
  0.6 3.4 %collective-permute-start = (bf16[1,128,128]{2,1,0:T(8,128)(2,1)}, bf16[1,128,128]{2,1,0:T(8,128)(2,1)S(1)}, u32[]{:S(2)}, u32[]{:S(2)}) collective-permute-start(bf16[1,128,128]{2,1,0:T(8,128)(2,1)} %param.7), channel_id=1, source_target_pairs={{0,128},{8,136},{16,144},{24,152},{32,160},{40,168},{48,176},{56,1... | collective-permute-start | bytes 98312 | tf_op jit(solution)/shard_map/ppermute | solution.py:294
  4.7 0.9 %fusion = bf16[1,448,128]{2,1,0:T(8,128)(2,1)S(1)} fusion(bf16[1,128,448]{1,2,0:T(8,128)(2,1)} %param.8, pred[128]{0:T(512)(128)(4,1)S(1)} %iota_compare_fusion), kind=kLoop, calls=%fused_computation.8 | loop fusion | flops 57344 | bytes 229504 | tf_op jit(solution)/shard_map/broadcast_in_dim | solution.py:298
  5.6 0.1 collective-permute-start.3
  5.7 5.5 %collective-permute-start.10 = (f32[1,32,512]{2,1,0:T(8,128)}, f32[1,32,512]{2,1,0:T(8,128)S(1)}, u32[]{:S(2)}, u32[]{:S(2)}) collective-permute-start(f32[1,32,512]{2,1,0:T(8,128)} %bitcast.15), channel_id=1, source_target_pairs={{0,4},{1,5},{2,6},{3,7},{4,0},{5,1},{6,2},{7,3},{8,12},{9,13},{10,... | collective-permute-start | bytes 196616 | tf_op jit(solution)/shard_map/ppermute | solution.py:294
  11.2 0.0 copy-done
  11.2 0.7 copy.10.words_ref
  11.9 0.6 pad_add_fusion.place_ref
  12.5 3.7 %sort_coords.1 = (s32[128,256]{1,0:T(8,128)}, bf16[256,4096]{1,0:T(8,128)(2,1)}, bf16[32,4096]{1,0:T(8,128)(2,1)}, s32[8,128]{1,0:T(8,128)}) custom-call(s32[32,128]{1,0:T(8,128)} %bitcast.19, s32[32,128]{1,0:T(8,128)} %bitcast.20), custom_call_target="tpu_custom_call" | custom-call | flops 1000000000 | bytes 3000000 | tf_op jit(solution)/shard_map/sort_coords/pallas_call | solution.py:99
  16.2 2.5 %sign_table.1.sign_ref = f32[4,448,128]{2,1,0:T(8,128)} custom-call(s32[2]{0:T(128)} %pad_add_fusion.place_ref, s32[128,64]{1,0:T(8,128)} %copy.10.words_ref), custom_call_target="tpu_custom_call" | custom-call | flops 1000000000 | bytes 1000000 | tf_op jit(solution)/shard_map/sign_table/pallas_call | solution.py:172
  18.8 0.0 copy-start.7
  18.8 0.0 copy-start.6
  18.8 5.2 %coord_signs.1 = (bf16[24,128,256]{2,1,0:T(8,128)(2,1)}, f32[24,64,256]{2,1,0:T(8,128)}, f32[24,32,256]{2,1,0:T(8,128)}) custom-call(s32[2]{0:T(128)} %pad_add_fusion.place_ref, s32[128,256]{1,0:T(8,128)} %get-tuple-element.10.sorted_ref), custom_call_target="tpu_custom_call" | custom-call | flops 1000000000 | bytes 4000000 | tf_op jit(solution)/shard_map/coord_signs/pallas_call | solution.py:135
  24.0 0.0 copy-start.1
  24.0 0.0 copy-start.2
  24.0 0.0 copy-start.5
  24.0 0.0 collective-permute-done
  24.0 0.0 copy-done.7
  24.0 1.1 %collective-permute-start.1 = (bf16[2,128,128]{2,1,0:T(8,128)(2,1)S(1)}, bf16[2,128,128]{2,1,0:T(8,128)(2,1)S(1)}, u32[]{:S(2)}, u32[]{:S(2)}) collective-permute-start(bf16[2,128,128]{2,1,0:T(8,128)(2,1)S(1)} %pad_maximum_fusion.7), channel_id=1, source_target_pairs={{0,64},{8,72},{16,80},{24,88},{32,96},{40,104},{48,112},{56,120},{... | collective-permute-start | bytes 196616 | tf_op jit(solution)/shard_map/ppermute | solution.py:294
  25.1 0.0 collective-permute-done.10
  25.1 0.0 copy-done.6
  25.2 0.5 collective-permute-start.11
  25.7 2.7 %collective-permute-done.1 = bf16[2,128,128]{2,1,0:T(8,128)(2,1)S(1)} collective-permute-done((bf16[2,128,128]{2,1,0:T(8,128)(2,1)S(1)}, bf16[2,128,128]{2,1,0:T(8,128)(2,1)S(1)}, u32[]{:S(2)}, u32[]{:S(2)}) %collective-permute-start.1) | collective-permute-done | bytes 65568 | tf_op jit(solution)/shard_map/ppermute | solution.py:294
  28.4 2.8 %collective-permute-start.2 = (bf16[4,128,128]{2,1,0:T(8,128)(2,1)S(1)}, bf16[4,128,128]{2,1,0:T(8,128)(2,1)S(1)}, u32[]{:S(2)}, u32[]{:S(2)}) collective-permute-start(bf16[4,128,128]{2,1,0:T(8,128)(2,1)S(1)} %pad_maximum_fusion.5), channel_id=1, source_target_pairs={{0,48},{8,56},{16,32},{24,40},{32,16},{40,24},{48,0},{56,8},{64,11... | collective-permute-start | bytes 393224 | tf_op jit(solution)/shard_map/ppermute | solution.py:294
  31.2 0.0 collective-permute-done.3
  31.3 0.3 collective-permute-start.4
  31.6 0.0 collective-permute-done.11
  31.6 1.7 %collective-permute-start.12 = (f32[4,32,512]{2,1,0:T(8,128)S(1)}, f32[4,32,512]{2,1,0:T(8,128)S(1)}, u32[]{:S(2)}, u32[]{:S(2)}) collective-permute-start(f32[4,32,512]{2,1,0:T(8,128)S(1)} %pad_maximum_fusion.3), channel_id=1, source_target_pairs={{0,3},{1,2},{2,1},{3,0},{4,7},{5,6},{6,5},{7,4},{8,11},{9,10},{10,... | collective-permute-start | bytes 786440 | tf_op jit(solution)/shard_map/ppermute | solution.py:294
  33.3 1.4 %collective-permute-done.2 = bf16[4,128,128]{2,1,0:T(8,128)(2,1)S(1)} collective-permute-done((bf16[4,128,128]{2,1,0:T(8,128)(2,1)S(1)}, bf16[4,128,128]{2,1,0:T(8,128)(2,1)S(1)}, u32[]{:S(2)}, u32[]{:S(2)}) %collective-permute-start.2) | collective-permute-done | bytes 131104 | tf_op jit(solution)/shard_map/ppermute | solution.py:294
  34.7 2.9 %collective-permute-done.4 = bf16[2,448,128]{2,1,0:T(8,128)(2,1)S(1)} collective-permute-done((bf16[2,448,128]{2,1,0:T(8,128)(2,1)S(1)}, bf16[2,448,128]{2,1,0:T(8,128)(2,1)S(1)}, u32[]{:S(2)}, u32[]{:S(2)}) %collective-permute-start.4) | collective-permute-done | bytes 229408 | tf_op jit(solution)/shard_map/ppermute | solution.py:294
  37.6 0.0 copy-done.1
  37.6 0.0 copy-done.2
  37.7 0.0 copy-done.5
  37.7 0.0 copy-start.3
  37.7 1.4 %copy-done.3 = f32[24,64,256]{2,1,0:T(8,128)S(1)} copy-done((f32[24,64,256]{2,1,0:T(8,128)S(1)}, f32[24,64,256]{2,1,0:T(8,128)}, u32[]{:S(2)}) %copy-start.3) | copy-done | bytes 1572888
  39.1 0.0 copy-start.4
  39.1 1.1 %copy-done.4 = f32[24,32,256]{2,1,0:T(8,128)S(1)} copy-done((f32[24,32,256]{2,1,0:T(8,128)S(1)}, f32[24,32,256]{2,1,0:T(8,128)}, u32[]{:S(2)}) %copy-start.4) | copy-done | bytes 786456
  40.2 11.9 %partial_sums.1 = f32[24,256]{1,0:T(8,128)S(1)} custom-call(s32[8,128]{1,0:T(8,128)S(1)} %copy-done.5, bf16[8,128,128]{2,1,0:T(8,128)(2,1)S(1)} %pad_maximum_fusion.2.a_ref, bf16[4,448,128]{2,1,0:T(8,128)(2,1)S(1)} %pad_maximum_fusion.1.g_ref, f32[4,448,128]{2,1,0:T(8,128)S(1)} %copy-done.1, bf16[24,128,256]{2,1,0:T(8,128)(2,1)S(1)} %copy-done.2, ...), custom_call_target="tpu_custom_call" | custom-call | flops 10000000000 | bytes 10000000 | tf_op jit(solution)/shard_map/partial_sums/pallas_call | solution.py:237
  52.1 0.1 collective-permute-start.5
  52.2 1.2 %collective-permute-done.5 = f32[24,256]{1,0:T(8,128)S(1)} collective-permute-done((f32[24,256]{1,0:T(8,128)S(1)}, f32[24,256]{1,0:T(8,128)S(1)}, u32[]{:S(2)}, u32[]{:S(2)}) %collective-permute-start.5) | collective-permute-done | bytes 24608 | tf_op jit(solution)/shard_map/ppermute | solution.py:294
  53.4 0.3 collective-permute-start.6
  53.7 3.5 %collective-permute-done.6 = f32[24,256]{1,0:T(8,128)S(1)} collective-permute-done((f32[24,256]{1,0:T(8,128)S(1)}, f32[24,256]{1,0:T(8,128)S(1)}, u32[]{:S(2)}, u32[]{:S(2)}) %collective-permute-start.6) | collective-permute-done | bytes 24608 | tf_op jit(solution)/shard_map/ppermute | solution.py:294
  57.2 0.5 collective-permute-start.7
  57.7 4.6 %collective-permute-done.7 = f32[24,256]{1,0:T(8,128)S(1)} collective-permute-done((f32[24,256]{1,0:T(8,128)S(1)}, f32[24,256]{1,0:T(8,128)S(1)}, u32[]{:S(2)}, u32[]{:S(2)}) %collective-permute-start.7) | collective-permute-done | bytes 24608 | tf_op jit(solution)/shard_map/ppermute | solution.py:294
  62.3 1.0 %collective-permute-start.8 = (f32[24,256]{1,0:T(8,128)S(1)}, f32[24,256]{1,0:T(8,128)S(1)}, u32[]{:S(2)}, u32[]{:S(2)}) collective-permute-start(f32[24,256]{1,0:T(8,128)S(1)} %add.20), channel_id=1, source_target_pairs={{0,64},{8,72},{16,80},{24,88},{32,96},{40,104},{48,112},{56,120},{... | collective-permute-start | bytes 73736 | tf_op jit(solution)/shard_map/ppermute | solution.py:294
  63.3 2.8 %collective-permute-done.8 = f32[24,256]{1,0:T(8,128)S(1)} collective-permute-done((f32[24,256]{1,0:T(8,128)S(1)}, f32[24,256]{1,0:T(8,128)S(1)}, u32[]{:S(2)}, u32[]{:S(2)}) %collective-permute-start.8) | collective-permute-done | bytes 24608 | tf_op jit(solution)/shard_map/ppermute | solution.py:294
  66.1 0.0 copy-start.8
  66.1 1.7 %collective-permute-start.9 = (f32[24,256]{1,0:T(8,128)S(1)}, f32[24,256]{1,0:T(8,128)S(1)}, u32[]{:S(2)}, u32[]{:S(2)}) collective-permute-start(f32[24,256]{1,0:T(8,128)S(1)} %add.21.mine_ref), channel_id=1, source_target_pairs={{0,128},{8,136},{16,144},{24,152},{32,160},{40,168},{48,176},{56,1... | collective-permute-start | bytes 73736 | tf_op jit(solution)/shard_map/ppermute | solution.py:294
  67.7 0.0 collective-permute-done.12
  67.7 0.8 %pad_maximum_fusion.q_ref = f32[8,32,512]{2,1,0:T(8,128)} fusion(f32[4,32,512]{2,1,0:T(8,128)S(1)} %collective-permute-done.12, f32[2,32,512]{2,1,0:T(8,128)S(1)} %collective-permute-done.11, f32[1,32,512]{2,1,0:T(8,128)S(1)} %collective-permute-done.10, f32[1,32,512]{2,1,0:T(8,128)S(1)} %bitcast.18), kind=kLoop, calls=%fused_computation | loop fusion | flops 393216 | bytes 1048576 | tf_op jit(solution)/shard_map/concatenate | solution.py:300
  68.6 2.3 %collective-permute-done.9.other_ref = f32[24,256]{1,0:T(8,128)S(1)} collective-permute-done((f32[24,256]{1,0:T(8,128)S(1)}, f32[24,256]{1,0:T(8,128)S(1)}, u32[]{:S(2)}, u32[]{:S(2)}) %collective-permute-start.9) | collective-permute-done | bytes 24608 | tf_op jit(solution)/shard_map/ppermute | solution.py:294
  70.9 0.0 copy-start.9
  70.9 0.0 copy-done.8
  70.9 0.6 copy-done.9
  71.5 3.0 %finish.1 = (f32[1,4096]{1,0:T(1,128)}, f32[1,32]{1,0:T(1,128)}) custom-call(s32[2]{0:T(128)} %pad_add_fusion.place_ref, f32[24,256]{1,0:T(8,128)} %copy-done.8, f32[24,256]{1,0:T(8,128)} %copy-done.9, bf16[256,4096]{1,0:T(8,128)(2,1)} %get-tuple-element.14.low_ref, bf16[32,4096]{1,0:T(8,128)(2,1)} %get-tuple-element.15.high_ref, ...), custom_call_target="tpu_custom_call" | custom-call | tf_op jit(solution)/shard_map/finish/pallas_call | solution.py:280
  (13 shorter events, 0.2 us)
Async XLA Ops:
  0.6 10.5 %copy-start = (s32[128,547]{0,1:T(8,128)S(1)}, s32[128,547]{0,1:T(8,128)}, u32[]{:S(2)}) copy-start(s32[128,547]{0,1:T(8,128)} %param.10) | copy-start | bytes 840196
  0.6 23.3 %collective-permute-start = (bf16[1,128,128]{2,1,0:T(8,128)(2,1)}, bf16[1,128,128]{2,1,0:T(8,128)(2,1)S(1)}, u32[]{:S(2)}, u32[]{:S(2)}) collective-permute-start(bf16[1,128,128]{2,1,0:T(8,128)(2,1)} %param.7), channel_id=1, source_target_pairs={{0,128},{8,136},{16,144},{24,152},{32,160},{40,168},{48,176},{56,1... | collective-permute-start | bytes 98312 | tf_op jit(solution)/shard_map/ppermute | solution.py:294
  5.6 25.7 %collective-permute-start.3 = (bf16[1,448,128]{2,1,0:T(8,128)(2,1)S(1)}, bf16[1,448,128]{2,1,0:T(8,128)(2,1)S(1)}, u32[]{:S(2)}, u32[]{:S(2)}) collective-permute-start(bf16[1,448,128]{2,1,0:T(8,128)(2,1)S(1)} %fusion), channel_id=1, source_target_pairs={{0,8},{8,0},{16,24},{24,16},{32,40},{40,32},{48,56},{56,48},{64,72... | collective-permute-start | bytes 344072 | tf_op jit(solution)/shard_map/ppermute | solution.py:294
  5.7 19.5 %collective-permute-start.10 = (f32[1,32,512]{2,1,0:T(8,128)}, f32[1,32,512]{2,1,0:T(8,128)S(1)}, u32[]{:S(2)}, u32[]{:S(2)}) collective-permute-start(f32[1,32,512]{2,1,0:T(8,128)} %bitcast.15), channel_id=1, source_target_pairs={{0,4},{1,5},{2,6},{3,7},{4,0},{5,1},{6,2},{7,3},{8,12},{9,13},{10,... | collective-permute-start | bytes 196616 | tf_op jit(solution)/shard_map/ppermute | solution.py:294
  18.8 5.2 %copy-start.7 = (bf16[1,128,128]{2,1,0:T(8,128)(2,1)S(1)}, bf16[1,128,128]{2,1,0:T(8,128)(2,1)}, u32[]{:S(2)}) copy-start(bf16[1,128,128]{2,1,0:T(8,128)(2,1)} %param.7) | copy-start | bytes 98308
  18.8 6.4 %copy-start.6 = (f32[32,512]{1,0:T(8,128)S(1)}, f32[32,512]{1,0:T(8,128)}, u32[]{:S(2)}) copy-start(f32[32,512]{1,0:T(8,128)} %param.13) | copy-start | bytes 196612
  24.0 13.7 %copy-start.1 = (f32[4,448,128]{2,1,0:T(8,128)S(1)}, f32[4,448,128]{2,1,0:T(8,128)}, u32[]{:S(2)}) copy-start(f32[4,448,128]{2,1,0:T(8,128)} %sign_table.1.sign_ref) | copy-start | bytes 2752516
  24.0 13.7 %copy-start.2 = (bf16[24,128,256]{2,1,0:T(8,128)(2,1)S(1)}, bf16[24,128,256]{2,1,0:T(8,128)(2,1)}, u32[]{:S(2)}) copy-start(bf16[24,128,256]{2,1,0:T(8,128)(2,1)} %get-tuple-element.11.u_ref) | copy-start | bytes 4718596
  24.0 13.7 %copy-start.5 = (s32[8,128]{1,0:T(8,128)S(1)}, s32[8,128]{1,0:T(8,128)}, u32[]{:S(2)}) copy-start(s32[8,128]{1,0:T(8,128)} %get-tuple-element.9.info_ref) | copy-start | bytes 12292
  24.0 4.4 %collective-permute-start.1 = (bf16[2,128,128]{2,1,0:T(8,128)(2,1)S(1)}, bf16[2,128,128]{2,1,0:T(8,128)(2,1)S(1)}, u32[]{:S(2)}, u32[]{:S(2)}) collective-permute-start(bf16[2,128,128]{2,1,0:T(8,128)(2,1)S(1)} %pad_maximum_fusion.7), channel_id=1, source_target_pairs={{0,64},{8,72},{16,80},{24,88},{32,96},{40,104},{48,112},{56,120},{... | collective-permute-start | bytes 196616 | tf_op jit(solution)/shard_map/ppermute | solution.py:294
  25.2 6.4 %collective-permute-start.11 = (f32[2,32,512]{2,1,0:T(8,128)S(1)}, f32[2,32,512]{2,1,0:T(8,128)S(1)}, u32[]{:S(2)}, u32[]{:S(2)}) collective-permute-start(f32[2,32,512]{2,1,0:T(8,128)S(1)} %pad_maximum_fusion.6), channel_id=1, source_target_pairs={{0,1},{1,0},{2,3},{3,2},{4,5},{5,4},{6,7},{7,6},{8,9},{9,8},{10,11... | collective-permute-start | bytes 393224 | tf_op jit(solution)/shard_map/ppermute | solution.py:294
  28.4 6.3 %collective-permute-start.2 = (bf16[4,128,128]{2,1,0:T(8,128)(2,1)S(1)}, bf16[4,128,128]{2,1,0:T(8,128)(2,1)S(1)}, u32[]{:S(2)}, u32[]{:S(2)}) collective-permute-start(bf16[4,128,128]{2,1,0:T(8,128)(2,1)S(1)} %pad_maximum_fusion.5), channel_id=1, source_target_pairs={{0,48},{8,56},{16,32},{24,40},{32,16},{40,24},{48,0},{56,8},{64,11... | collective-permute-start | bytes 393224 | tf_op jit(solution)/shard_map/ppermute | solution.py:294
  31.3 6.3 %collective-permute-start.4 = (bf16[2,448,128]{2,1,0:T(8,128)(2,1)S(1)}, bf16[2,448,128]{2,1,0:T(8,128)(2,1)S(1)}, u32[]{:S(2)}, u32[]{:S(2)}) collective-permute-start(bf16[2,448,128]{2,1,0:T(8,128)(2,1)S(1)} %pad_maximum_fusion.4), channel_id=1, source_target_pairs={{0,16},{8,24},{16,0},{24,8},{32,48},{40,56},{48,32},{56,40},{64,80... | collective-permute-start | bytes 688136 | tf_op jit(solution)/shard_map/ppermute | solution.py:294
  31.6 36.1 %collective-permute-start.12 = (f32[4,32,512]{2,1,0:T(8,128)S(1)}, f32[4,32,512]{2,1,0:T(8,128)S(1)}, u32[]{:S(2)}, u32[]{:S(2)}) collective-permute-start(f32[4,32,512]{2,1,0:T(8,128)S(1)} %pad_maximum_fusion.3), channel_id=1, source_target_pairs={{0,3},{1,2},{2,1},{3,0},{4,7},{5,6},{6,5},{7,4},{8,11},{9,10},{10,... | collective-permute-start | bytes 786440 | tf_op jit(solution)/shard_map/ppermute | solution.py:294
  37.7 1.4 %copy-start.3 = (f32[24,64,256]{2,1,0:T(8,128)S(1)}, f32[24,64,256]{2,1,0:T(8,128)}, u32[]{:S(2)}) copy-start(f32[24,64,256]{2,1,0:T(8,128)} %get-tuple-element.12.vl_ref) | copy-start | bytes 4718596
  39.1 1.1 %copy-start.4 = (f32[24,32,256]{2,1,0:T(8,128)S(1)}, f32[24,32,256]{2,1,0:T(8,128)}, u32[]{:S(2)}) copy-start(f32[24,32,256]{2,1,0:T(8,128)} %get-tuple-element.13.vj_ref) | copy-start | bytes 2359300
  52.1 1.3 %collective-permute-start.5 = (f32[24,256]{1,0:T(8,128)S(1)}, f32[24,256]{1,0:T(8,128)S(1)}, u32[]{:S(2)}, u32[]{:S(2)}) collective-permute-start(f32[24,256]{1,0:T(8,128)S(1)} %partial_sums.1), channel_id=1, source_target_pairs={{0,8},{8,0},{16,24},{24,16},{32,40},{40,32},{48,56},{56,48},{64,72... | collective-permute-start | bytes 73736 | tf_op jit(solution)/shard_map/ppermute | solution.py:294
  53.4 3.8 %collective-permute-start.6 = (f32[24,256]{1,0:T(8,128)S(1)}, f32[24,256]{1,0:T(8,128)S(1)}, u32[]{:S(2)}, u32[]{:S(2)}) collective-permute-start(f32[24,256]{1,0:T(8,128)S(1)} %add.18), channel_id=1, source_target_pairs={{0,16},{8,24},{16,0},{24,8},{32,48},{40,56},{48,32},{56,40},{64,80... | collective-permute-start | bytes 73736 | tf_op jit(solution)/shard_map/ppermute | solution.py:294
  57.2 5.0 %collective-permute-start.7 = (f32[24,256]{1,0:T(8,128)S(1)}, f32[24,256]{1,0:T(8,128)S(1)}, u32[]{:S(2)}, u32[]{:S(2)}) collective-permute-start(f32[24,256]{1,0:T(8,128)S(1)} %add.19), channel_id=1, source_target_pairs={{0,48},{8,56},{16,32},{24,40},{32,16},{40,24},{48,0},{56,8},{64,11... | collective-permute-start | bytes 73736 | tf_op jit(solution)/shard_map/ppermute | solution.py:294
  62.3 3.8 %collective-permute-start.8 = (f32[24,256]{1,0:T(8,128)S(1)}, f32[24,256]{1,0:T(8,128)S(1)}, u32[]{:S(2)}, u32[]{:S(2)}) collective-permute-start(f32[24,256]{1,0:T(8,128)S(1)} %add.20), channel_id=1, source_target_pairs={{0,64},{8,72},{16,80},{24,88},{32,96},{40,104},{48,112},{56,120},{... | collective-permute-start | bytes 73736 | tf_op jit(solution)/shard_map/ppermute | solution.py:294
  66.1 4.8 %copy-start.8 = (f32[24,256]{1,0:T(8,128)}, f32[24,256]{1,0:T(8,128)S(1)}, u32[]{:S(2)}) copy-start(f32[24,256]{1,0:T(8,128)S(1)} %add.21.mine_ref) | copy-start | bytes 73732
  66.1 4.8 %collective-permute-start.9 = (f32[24,256]{1,0:T(8,128)S(1)}, f32[24,256]{1,0:T(8,128)S(1)}, u32[]{:S(2)}, u32[]{:S(2)}) collective-permute-start(f32[24,256]{1,0:T(8,128)S(1)} %add.21.mine_ref), channel_id=1, source_target_pairs={{0,128},{8,136},{16,144},{24,152},{32,160},{40,168},{48,176},{56,1... | collective-permute-start | bytes 73736 | tf_op jit(solution)/shard_map/ppermute | solution.py:294
  70.9 0.6 copy-start.9

commit v2 on v1

v2 whole, which is shorter than its diff:
```python
import math

import jax
import jax.numpy as jnp
from jax import lax
from jax.experimental import pallas as pl
from jax.experimental.pallas import tpu as pltpu
from jax.sharding import PartitionSpec as P

DIN = 4096
DPAD = 16384
PROJ = 4096
TOK = 128
COLS = 448
RUNS = COLS // 64
ROW_GROUPS = 8
COL_GROUPS = 8
GROUPS = ROW_GROUPS * COL_GROUPS
BLK = 128
MAXB = 96
UNROLL = 16
PIECES = 4
RUNS_HERE = PIECES * RUNS

ROW_STEPS = (16, 8, 6)
COL_STEPS = (1, 2)
SUM_STEPS = (1, 2, 6, 8, 16)
EX_STEPS = (4, 1, 3)

F32 = jnp.float32
BF16 = jnp.bfloat16
I32 = jnp.int32
NT = (((1,), (1,)), ((), ()))


def iota(shape, dim):
    return lax.broadcasted_iota(I32, shape, dim)


def parity(bits):
    bits = bits ^ (bits >> 4)
    bits = bits ^ (bits >> 2)
    bits = bits ^ (bits >> 1)
    return bits & 1


def parity3(bits):
    return (bits ^ (bits >> 1) ^ (bits >> 2)) & 1


def sign_of(bit):
    return (1 - 2 * bit).astype(F32)


def one_hot(cond):
    return jnp.where(cond, 1.0, 0.0)


def cost(microseconds):
    return pl.CostEstimate(
        flops=int(microseconds * 10**9), bytes_accessed=10**6, transcendentals=0
    )


def rank_kernel(ints_ref, after_ref, place_ref, info_ref, hot_ref, count_ref):
    coord = ints_ref[0:32, :]
    block_row = coord >> 21
    key = (
        ((coord >> 3) & 7)
        | (((block_row >> 4) & 1) << 3)
        | (((block_row >> 3) & 1) << 4)
        | ((((block_row >> 1) ^ (block_row >> 2)) & 1) << 5)
    )
    for i in range(32):
        hot_ref[GROUPS * i : GROUPS * i + GROUPS, :] = one_hot(
            iota((GROUPS, 128), 0) == key[i : i + 1]
        ).astype(BF16)
    lane = iota((128, 256), 1)
    upto = one_hot((iota((128, 256), 0) <= lane) | (lane >= 128)).astype(BF16)
    count_ref[...] = jnp.dot(hot_ref[...], upto, preferred_element_type=F32)
    total = jnp.zeros((GROUPS, 128), F32)
    for i in range(32):
        here = slice(GROUPS * i, GROUPS * i + GROUPS)
        count_ref[here, 0:128] = count_ref[here, 0:128] + total
        total = total + count_ref[here, 128:256]
    blocks = ((total.astype(I32) + (BLK - 1)) >> 7).astype(F32)
    earlier = one_hot(iota((GROUPS, GROUPS), 1) < iota((GROUPS, GROUPS), 0)).astype(BF16)
    base = jnp.dot(earlier, blocks.astype(BF16), preferred_element_type=F32)
    upto_here = base + blocks
    ended = one_hot(upto_here <= iota((GROUPS, 128), 1).astype(F32))
    owner = jnp.minimum(jnp.sum(ended, axis=0, keepdims=True), GROUPS - 1.0).astype(I32)
    used = upto_here[GROUPS - 1 : GROUPS].astype(I32)
    info_ref[...] = jnp.concatenate([owner, used, jnp.zeros((6, 128), I32)], axis=0)
    base = base * float(BLK) - 1.0
    for i in range(32):
        here = slice(GROUPS * i, GROUPS * i + GROUPS)
        spot = hot_ref[here, :].astype(F32) * (count_ref[here, 0:128] + base)
        place_ref[i : i + 1, :] = jnp.sum(spot, axis=0, keepdims=True).astype(I32)

def rank_coords(ints, after):
    return pl.pallas_call(
        rank_kernel,
        out_shape=(
            jax.ShapeDtypeStruct((32, 128), I32),
            jax.ShapeDtypeStruct((8, 128), I32),
        ),
        in_specs=[pl.BlockSpec(memory_space=pltpu.VMEM), pl.BlockSpec(memory_space=pl.ANY)],
        scratch_shapes=[
            pltpu.VMEM((GROUPS * 32, 128), BF16),
            pltpu.VMEM((GROUPS * 32, 256), F32),
        ],
        compiler_params=pltpu.CompilerParams(vmem_limit_bytes=8 * 2**20),
        cost_estimate=cost(1),
        name="rank_coords",
    )(ints, after)


def sort_kernel(
    coord_ref, place_ref, after_ref, after_too_ref, sorted_ref, low_ref, high_ref, value_ref
):
    for i in range(32):
        at = slice(128 * i, 128 * i + 128)
        spot, coord = place_ref[i : i + 1, :], coord_ref[i : i + 1, :]
        low_ref[:, at] = one_hot(iota((BLK, 128), 0) == (spot & (BLK - 1))).astype(BF16)
        high = one_hot(iota((MAXB, 128), 0) == (spot >> 7))
        high_ref[:, at] = high.astype(BF16)
        fields = ((coord >> 14) & 127, (coord >> 6) & 255, ((coord >> 21) << 3) | (coord & 7))
        for n, field in enumerate(fields):
            value_ref[MAXB * n : MAXB * n + MAXB, at] = (high * field.astype(F32)).astype(BF16)
    sorted_ref[...] = lax.dot_general(
        value_ref[...], low_ref[...], NT, preferred_element_type=F32
    ).astype(I32)


def sort_coords(coord, place, after, after_too):
    vmem = pl.BlockSpec(memory_space=pltpu.VMEM)
    return pl.pallas_call(
        sort_kernel,
        out_shape=(
            jax.ShapeDtypeStruct((3 * MAXB, BLK), I32),
            jax.ShapeDtypeStruct((BLK, PROJ), BF16),
            jax.ShapeDtypeStruct((MAXB, PROJ), BF16),
        ),
        in_specs=[vmem] * 2 + [pl.BlockSpec(memory_space=pl.ANY)] * 2,
        scratch_shapes=[pltpu.VMEM((3 * MAXB, PROJ), BF16)],
        compiler_params=pltpu.CompilerParams(vmem_limit_bytes=8 * 2**20),
        cost_estimate=cost(2),
        name="sort_coords",
    )(coord, place, after, after_too)


def coord_signs_kernel(info_ref, sorted_ref, after_ref, u_ref, vl_ref, vj_ref):
    feat = lax.axis_index("feat")
    run = iota((32, BLK), 0)
    piece = (run * 37) >> 8
    run = RUNS * (feat ^ piece) + (run - RUNS * piece)
    eight = iota((8, BLK), 0)

    def step(i, carry):
        for n in range(UNROLL):
            b = i * UNROLL + n
            row = sorted_ref[pl.ds(b, 1), :]
            col_high = sorted_ref[pl.ds(MAXB + b, 1), :]
            rest = sorted_ref[pl.ds(2 * MAXB + b, 1), :]
            column = [sign_of(parity3(eight & row))]
            for bit in range(3, 7):
                turn = sign_of((row >> bit) & 1)
                column = column + [part * turn for part in column]
            u_ref[b] = jnp.concatenate(column, axis=0).astype(BF16)
            flip = parity((rest >> 3) & feat)
            vl_ref[b] = sign_of(parity3(eight & rest) ^ flip) * (1.0 / math.sqrt(DIN * DPAD))
            vj_ref[b] = sign_of(parity(run & col_high))
        return carry

    lax.fori_loop(0, (info_ref[1, 0] + (UNROLL - 1)) // UNROLL, step, 0)


def coord_signs(info, sorted_fields, after):
    return pl.pallas_call(
        coord_signs_kernel,
        out_shape=(
            jax.ShapeDtypeStruct((MAXB, 128, BLK), BF16),
            jax.ShapeDtypeStruct((MAXB, 8, BLK), F32),
            jax.ShapeDtypeStruct((MAXB, 32, BLK), F32),
        ),
        in_specs=[
            pl.BlockSpec(memory_space=pltpu.SMEM),
            pl.BlockSpec(memory_space=pltpu.VMEM),
            pl.BlockSpec(memory_space=pl.ANY),
        ],
        compiler_params=pltpu.CompilerParams(vmem_limit_bytes=8 * 2**20),
        cost_estimate=cost(3),
        name="coord_signs",
    )(info, sorted_fields, after)


def table_kernel(words_ref, after_ref, sign_ref):
    feat = lax.axis_index("feat")
    first_word = ((PIECES * COLS * (feat >> 2)) * 34953) >> 20
    words = words_ref[pl.ds(first_word, 64), :]
    octets = jnp.concatenate(
        [((words >> (8 * p)) & 255).astype(F32) for p in range(4)], axis=0
    ).astype(BF16)
    for e in range(PIECES):
        col = COLS * (feat ^ e) + iota((COLS, 128), 0)
        word = (col * 34953) >> 20
        bit = col - 30 * word
        target = ((bit >> 3) << 6) + (word - first_word)
        lane = iota((COLS, 128), 1)
        pick = jnp.concatenate(
            [one_hot(lane == target), one_hot(lane + 128 == target)], axis=1
        ).astype(BF16)
        octet = jnp.dot(pick, octets, preferred_element_type=F32).astype(I32)
        sign_ref[COLS * e : COLS * e + COLS, :] = sign_of((octet >> (bit & 7)) & 1)


def sign_table(words, after):
    return pl.pallas_call(
        table_kernel,
        out_shape=jax.ShapeDtypeStruct((PIECES * COLS, 128), F32),
        in_specs=[pl.BlockSpec(memory_space=pltpu.VMEM), pl.BlockSpec(memory_space=pl.ANY)],
        compiler_params=pltpu.CompilerParams(vmem_limit_bytes=8 * 2**20),
        cost_estimate=cost(2),
        name="sign_table",
    )(words, after)


def butterflies(parts):
    parts = list(parts)
    for bit in (1, 2, 4):
        for i in range(len(parts)):
            if not i & bit:
                one, two = parts[i], parts[i | bit]
                parts[i], parts[i | bit] = one + two, one - two
    return parts


def split(value):
    high = value.astype(BF16)
    return high, (value - high.astype(F32)).astype(BF16)


def main_kernel(
    info_ref, counts_ref, a_ref, g_ref, sign_ref, u_ref, vl_ref, vj_ref, low_ref, high_ref,
    out_ref, mixed_ref, signed_ref, block_ref,
):
    for first in range(0, TOK, 32):
        rows = slice(first, first + 32)
        parts = [a_ref[i, rows, :].astype(F32) for i in range(ROW_GROUPS)]
        live = first + iota((32, 128), 0) < counts_ref[0:1, 0:1]
        parts = [jnp.where(live, part, 0.0) for part in butterflies(parts)]
        for i in range(ROW_GROUPS):
            high, low = split(parts[i])
            mixed_ref[rows, 128 * i : 128 * i + 128] = high
            mixed_ref[TOK + first : TOK + first + 32, 128 * i : 128 * i + 128] = low
    tile = 2 * COLS
    for first in range(0, PIECES * COLS, tile):
        grads = g_ref[first : first + tile, :]
        grads = jnp.concatenate([grads, grads], axis=1)
        for pair in range(ROW_GROUPS // 2):
            outer = jnp.dot(
                grads, mixed_ref[:, 256 * pair : 256 * pair + 256], preferred_element_type=F32
            )
            for half in range(2):
                group = COL_GROUPS * (2 * pair + half)
                for at in range(0, tile, 128):
                    signed = (
                        outer[at : at + 128, 128 * half : 128 * half + 128]
                        * sign_ref[first + at : first + at + 128, :]
                    )
                    runs = [
                        butterflies(
                            [signed[64 * r + 8 * h : 64 * r + 8 * h + 8] for h in range(COL_GROUPS)]
                        )
                        for r in range(2)
                    ]
                    to = (first + at) // 8
                    for h in range(COL_GROUPS):
                        high, low = split(jnp.concatenate([runs[0][h], runs[1][h]], axis=0))
                        signed_ref[group + h, to : to + 16, 0:128] = high
                        signed_ref[group + h, to : to + 16, 128:256] = low
    block_ref[...] = jnp.zeros_like(block_ref)

    def step(i, carry):
        for n in range(UNROLL):
            b = i * UNROLL + n
            weights = jnp.concatenate([u_ref[b], u_ref[b]], axis=0)
            rows = jnp.dot(signed_ref[info_ref[0, b]], weights, preferred_element_type=F32)
            total = vj_ref[b, 0:1, :] * rows[0:8]
            for j in range(1, RUNS_HERE):
                total = total + vj_ref[b, j : j + 1, :] * rows[8 * j : 8 * j + 8]
            block_ref[pl.ds(b, 1), :] = jnp.sum(total * vl_ref[b], axis=0, keepdims=True)
        return carry

    lax.fori_loop(0, (info_ref[1, 0] + (UNROLL - 1)) // UNROLL, step, 0)
    pair = jnp.concatenate(split(block_ref[...]), axis=1)
    for first in range(0, PROJ, 512):
        at = slice(first, first + 512)
        low = low_ref[:, at]
        spread = jnp.dot(pair, jnp.concatenate([low, low], axis=0), preferred_element_type=F32)
        out_ref[:, at] = jnp.sum(spread * high_ref[:, at].astype(F32), axis=0, keepdims=True)


def partial_sums(info, counts, acts, grads, signs, u, vl, vj, low, high):
    vmem = pl.BlockSpec(memory_space=pltpu.VMEM)
    return pl.pallas_call(
        main_kernel,
        out_shape=jax.ShapeDtypeStruct((1, PROJ), F32),
        in_specs=[pl.BlockSpec(memory_space=pltpu.SMEM)] + [vmem] * 9,
        out_specs=vmem,
        scratch_shapes=[
            pltpu.VMEM((2 * TOK, ROW_GROUPS * 128), BF16),
            pltpu.VMEM((GROUPS, RUNS_HERE * 8, 256), BF16),
            pltpu.VMEM((MAXB, BLK), F32),
        ],
        cost_estimate=cost(7),
        compiler_params=pltpu.CompilerParams(vmem_limit_bytes=16 * 2**20),
        name="partial_sums",
    )(info, counts, acts, grads, signs, u, vl, vj, low, high)


def finish_kernel(mine_ref, other_ref, q0_ref, q1_ref, q2_ref, q3_ref, proj_ref, score_ref, row_ref):
    ex = lax.axis_index("ex")
    proj = mine_ref[...] + other_ref[...]
    proj_ref[...] = proj
    for s in range(8):
        row_ref[s : s + 1, :] = proj[:, 512 * s : 512 * s + 512]
    acc = q0_ref[...] * row_ref[pl.ds(ex, 1), :]
    order = [0]
    for step, ref in zip(EX_STEPS, (q1_ref, q2_ref, q3_ref)):
        fresh = [d ^ step for d in order]
        for n, d in enumerate(fresh):
            acc = acc + ref[n] * row_ref[pl.ds(ex ^ d, 1), :]
        order = order + fresh
    acc = (acc[:, 0:128] + acc[:, 128:256]) + (acc[:, 256:384] + acc[:, 384:512])
    scores = lax.dot_general(
        jnp.ones((8, 128), F32), acc, NT, precision=lax.Precision.HIGHEST, preferred_element_type=F32
    )
    score_ref[...] = scores[0:1] * (1.0 / math.sqrt(PROJ))


def finish(mine, other, queries):
    vmem = pl.BlockSpec(memory_space=pltpu.VMEM)
    return pl.pallas_call(
        finish_kernel,
        out_shape=(
            jax.ShapeDtypeStruct((1, PROJ), F32),
            jax.ShapeDtypeStruct((1, 32), F32),
        ),
        in_specs=[vmem] * 6,
        out_specs=(vmem, vmem),
        scratch_shapes=[pltpu.VMEM((8, 512), F32)],
        compiler_params=pltpu.CompilerParams(vmem_limit_bytes=4 * 2**20),
        cost_estimate=cost(1),
        name="finish",
    )(mine, other, *queries)


def swap(value, axis, size, step):
    return lax.ppermute(value, axis, [(i, i ^ step) for i in range(size)])


def body(activations, output_grads, counts, sign_words, coord_row, coord_col, queries):
    grads = output_grads[0].T
    got = swap(activations, "feat", 32, ROW_STEPS[0])
    got_grads = swap(grads, "feat", 32, COL_STEPS[0])
    own = jnp.concatenate([activations[0], grads], axis=0)
    ints = jnp.concatenate(
        [(coord_row << 14) | coord_col, jnp.broadcast_to(counts, (8 * 128,))]
    ).reshape(40, 128)
    own, ints = lax.optimization_barrier((own, ints))
    place, info = rank_coords(ints, own)
    own, got, got_grads, _ = lax.optimization_barrier((own, got, got_grads, place))
    acts = jnp.concatenate([own[None, :TOK], got], axis=0)
    grads = jnp.concatenate([own[TOK:], got_grads], axis=0)
    got = swap(acts, "feat", 32, ROW_STEPS[1])
    got_grads = swap(grads, "feat", 32, COL_STEPS[1])
    signs = sign_table(sign_words.T, grads)
    sorted_fields, low, high = sort_coords(ints, place, grads, signs)
    acts, got, _ = lax.optimization_barrier((acts, got, sorted_fields))
    acts = jnp.concatenate([acts, got], axis=0)
    got = swap(acts, "feat", 32, ROW_STEPS[2])
    u, vl, vj = coord_signs(info, sorted_fields, acts)
    q, _ = lax.optimization_barrier((queries[None], acts))
    got_q = [swap(q, "ex", 8, EX_STEPS[0])]
    q = jnp.concatenate([q, got_q[-1]], axis=0)
    q, _ = lax.optimization_barrier((q, u))
    got_q.append(swap(q, "ex", 8, EX_STEPS[1]))
    q = jnp.concatenate([q, got_q[-1]], axis=0)
    acts = jnp.concatenate([acts, got], axis=0)
    grads = jnp.concatenate([grads, got_grads], axis=0)
    total = partial_sums(info, ints[32:], acts, grads, signs, u, vl, vj, low, high)
    for n, step in enumerate(SUM_STEPS[:-1]):
        total = total + swap(total, "feat", 32, step)
        if n == 0:
            q, total = lax.optimization_barrier((q, total))
            got_q.append(swap(q, "ex", 8, EX_STEPS[2]))
    other = swap(total, "feat", 32, SUM_STEPS[-1])
    return finish(total, other, [queries] + got_q)


def solution(mesh):
    return jax.shard_map(
        body,
        mesh=mesh,
        in_specs=(
            P("ex", None, "feat"),
            P("ex", None, "feat"),
            P("ex"),
            P(),
            P(),
            P(),
            P("feat", "ex"),
        ),
        out_specs=(P("ex", None), P("ex", "feat")),
        check_vma=False,
    )
```

time: 74.4 us -> 52.8 us (0.71)
  Pallas kernels: 26.4 us -> 11.6 us
  waiting for transfers between devices: 21.4 us -> 14.5 us
  starting transfers between devices: 18.9 us -> 22.9 us
  local copies, waits for them, and re-layouts: 3.9 us -> 0.05 us
    pallas_call x3 -> x4, Pallas kernels: 18.1 us -> 9.24 us  [the longest x1 6.23 us: partial_sums(): pl.pallas_call(main_kernel, out_shape=jax.ShapeDtypeStruct((1, PROJ), F32...]
    ppermute x13, waiting for transfers between devices: 21.4 us -> 14.5 us  [swap(): return lax.ppermute(value, axis, [(i, i ^ step) for i in range(size)])]
    ppermute x13, starting transfers between devices: 18.9 us -> 22.9 us  [swap(): return lax.ppermute(value, axis, [(i, i ^ step) for i in range(size)])]
    unnamed x21 -> x5, local copies, waits for them, and re-layouts: 3.89 us -> 0.02 us
    pallas_call x1, Pallas kernels: 5.22 us -> 1.67 us  [coord_signs(): pl.pallas_call(coord_signs_kernel, out_shape=(jax.ShapeDtypeStruct((MAXB,...]
    pallas_call x1, Pallas kernels: 3.02 us -> 0.7 us  [finish(): pl.pallas_call(finish_kernel, out_shape=(jax.ShapeDtypeStruct((1, PROJ),...]
    broadcast_in_dim x1 -> x0, other arithmetic: 0.91 us -> none  [gather_by(): value = value[None]]
  transfers between devices with their start and end apart: 13 -> 13, of which waited for: 8 -> 6; matrix products, arithmetic and copies ran while one was open for 4% -> 4% of each run, Pallas kernels for 31% -> 21%
where the time goes in v2:
time: 52.8 us; the launch traced here: 52.3 us
  starting transfers between devices  22.9 us (43%)
  waiting for transfers between devices  14.5 us (27%)
  Pallas kernels  11.6 us (22%)
  other arithmetic  1.85 us (4%)
  between operations  1.47 us (3%)
    ppermute x13, starting transfers between devices, swap(): return lax.ppermute(value, axis, [(i, i ^ step) for i in range(size)])  22.9 us
    ppermute x13, waiting for transfers between devices, swap(): return lax.ppermute(value, axis, [(i, i ^ step) for i in range(size)])  14.5 us
    pallas_call x1, Pallas kernels, partial_sums(): pl.pallas_call(main_kernel, out_shape=jax.ShapeDtypeStruct((1, PROJ), F32...  6.23 us
    pallas_call x1, Pallas kernels, coord_signs(): pl.pallas_call(coord_signs_kernel, out_shape=(jax.ShapeDtypeStruct((MAXB,...  1.67 us
    pallas_call x1, Pallas kernels, sort_coords(): pl.pallas_call(sort_kernel, out_shape=(jax.ShapeDtypeStruct((3 * MAXB, BL...  1.55 us
  transfers between devices with their start and end apart: 13, of which 6 were waited for; matrix products, arithmetic and copies ran while one was open for 4% of the time, Pallas kernels for 21%

profile of v2, /device:TPU:8, one launch (start us, length us, event | category | flops | bytes accessed | tf_op | source)
XLA Modules:
  0.0 52.3 jit_solution(2304424141578306013)
XLA Ops:
  0.6 0.0 copy-start.1
  0.6 3.4 %collective-permute-start = (bf16[1,128,128]{2,1,0:T(8,128)(2,1)}, bf16[1,128,128]{2,1,0:T(8,128)(2,1)S(1)}, u32[]{:S(2)}, u32[]{:S(2)}) collective-permute-start(bf16[1,128,128]{2,1,0:T(8,128)(2,1)} %param.7), channel_id=1, source_target_pairs={{0,128},{8,136},{16,144},{24,152},{32,160},{40,168},{48,176},{56,1... | collective-permute-start | bytes 98312 | tf_op jit(solution)/shard_map/ppermute | solution.py:360
  4.0 0.0 collective-permute-start.1
  4.7 0.9 %pad_maximum_fusion.4.after_ref = bf16[576,128]{1,0:T(8,128)(2,1)S(1)} fusion(bf16[448,128]{1,0:T(8,128)(2,1)} %bitcast.16, bf16[128,128]{1,0:T(8,128)(2,1)} %bitcast.17), kind=kLoop, calls=%fused_computation.4 | loop fusion | flops 294912 | bytes 294912 | tf_op jit(solution)/shard_map/concatenate | solution.py:367
  5.6 0.7 %shift-left_or_fusion = s32[4096]{0:T(1024)S(1)} fusion(s32[4096]{0:T(1024)} %param.12, s32[4096]{0:T(1024)} %param.11), kind=kLoop, calls=%fused_computation.9 | loop fusion | flops 8192 | bytes 49152 | tf_op jit(solution)/shard_map/or | solution.py:369
  6.3 0.8 %rank_coords.1 = (s32[32,128]{1,0:T(8,128)S(1)}, s32[8,128]{1,0:T(8,128)S(1)}) custom-call(s32[40,128]{1,0:T(8,128)S(1)} %pad_bitcast_fusion.ints_ref.coord_ref, bf16[576,128]{1,0:T(8,128)(2,1)S(1)} %pad_maximum_fusion.4.after_ref), custom_call_target="tpu_custom_call" | custom-call | flops 1000000000 | bytes 1000000 | tf_op jit(solution)/shard_map/rank_coords/pallas_call | solution.py:101
  7.1 0.0 collective-permute-done
  7.1 0.0 collective-permute-done.1
  7.2 2.0 %collective-permute-start.2 = (bf16[2,128,128]{2,1,0:T(8,128)(2,1)S(1)}, bf16[2,128,128]{2,1,0:T(8,128)(2,1)S(1)}, u32[]{:S(2)}, u32[]{:S(2)}) collective-permute-start(bf16[2,128,128]{2,1,0:T(8,128)(2,1)S(1)} %pad_maximum_fusion.6), channel_id=1, source_target_pairs={{0,64},{8,72},{16,80},{24,88},{32,96},{40,104},{48,112},{56,120},{... | collective-permute-start | bytes 196616 | tf_op jit(solution)/shard_map/ppermute | solution.py:360
  9.2 1.6 %collective-permute-start.6 = (bf16[896,128]{1,0:T(8,128)(2,1)S(1)}, bf16[896,128]{1,0:T(8,128)(2,1)S(1)}, u32[]{:S(2)}, u32[]{:S(2)}) collective-permute-start(bf16[896,128]{1,0:T(8,128)(2,1)S(1)} %pad_maximum_fusion.3.after_ref), channel_id=1, source_target_pairs={{0,16},{8,24},{16,0},{24,8},{32,48},{40,56},{48,32},{56,40},{64,80... | collective-permute-start | bytes 688136 | tf_op jit(solution)/shard_map/ppermute | solution.py:360
  10.8 0.0 copy-done.1
  10.8 0.7 %sign_table.1.after_too_ref.sign_ref = f32[1792,128]{1,0:T(8,128)S(1)} custom-call(s32[547,128]{1,0:T(8,128)S(1)} %bitcast.14, bf16[896,128]{1,0:T(8,128)(2,1)S(1)} %pad_maximum_fusion.3.after_ref), custom_call_target="tpu_custom_call" | custom-call | flops 2000000000 | bytes 1000000 | tf_op jit(solution)/shard_map/sign_table/pallas_call | solution.py:218
  11.5 0.0 copy-start
  11.5 1.6 %sort_coords.1 = (s32[288,128]{1,0:T(8,128)S(1)}, bf16[128,4096]{1,0:T(8,128)(2,1)S(1)}, bf16[96,4096]{1,0:T(8,128)(2,1)S(1)}) custom-call(s32[40,128]{1,0:T(8,128)S(1)} %pad_bitcast_fusion.ints_ref.coord_ref, s32[32,128]{1,0:T(8,128)S(1)} %get-tuple-element.23.place_ref, bf16[896,128]{1,0:T(8,128)(2,1)S(1)} %pad_maximum_fusion.3.after_ref, ...), custom_call_target="tpu_custom_call" | custom-call | flops 2000000000 | bytes 1000000 | tf_op jit(solution)/shard_map/sort_coords/pallas_call | solution.py:137
  13.0 0.0 collective-permute-done.2
  13.1 2.2 %collective-permute-start.5 = (bf16[4,128,128]{2,1,0:T(8,128)(2,1)S(1)}, bf16[4,128,128]{2,1,0:T(8,128)(2,1)S(1)}, u32[]{:S(2)}, u32[]{:S(2)}) collective-permute-start(bf16[4,128,128]{2,1,0:T(8,128)(2,1)S(1)} %constant_dynamic-update-slice_fusion.after_ref), channel_id=1, source_target_pairs={{0,48},{8,56},{16,32},{24,40},{32,16},{40,24},{48,0},{56,8},{64,11... | collective-permute-start | bytes 393224 | tf_op jit(solution)/shard_map/ppermute | solution.py:360
  15.2 0.0 copy-done
  15.3 4.9 %collective-permute-start.3 = (f32[1,32,512]{2,1,0:T(8,128)S(1)}, f32[1,32,512]{2,1,0:T(8,128)S(1)}, u32[]{:S(2)}, u32[]{:S(2)}) collective-permute-start(f32[1,32,512]{2,1,0:T(8,128)S(1)} %bitcast.12), channel_id=1, source_target_pairs={{0,4},{1,5},{2,6},{3,7},{4,0},{5,1},{6,2},{7,3},{8,12},{9,13},{10,... | collective-permute-start | bytes 196616 | tf_op jit(solution)/shard_map/ppermute | solution.py:360
  20.2 1.7 %coord_signs.1 = (bf16[96,128,128]{2,1,0:T(8,128)(2,1)S(1)}, f32[96,8,128]{2,1,0:T(8,128)S(1)}, f32[96,32,128]{2,1,0:T(8,128)S(1)}) custom-call(s32[8,128]{1,0:T(8,128)S(1)} %get-tuple-element.31.info_ref, s32[288,128]{1,0:T(8,128)S(1)} %get-tuple-element.27.sorted_ref, bf16[4,128,128]{2,1,0:T(8,128)(2,1)S(1)} %constant_dynamic-update-slice_fusion.after_ref), custom_call_target="tpu_custom_call" | custom-call | flops 3000000000 | bytes 1000000 | tf_op jit(solution)/shard_map/coord_signs/pallas_call | solution.py:179
  21.9 1.7 %collective-permute-done.3.q1_ref = f32[1,32,512]{2,1,0:T(8,128)S(1)} collective-permute-done((f32[1,32,512]{2,1,0:T(8,128)S(1)}, f32[1,32,512]{2,1,0:T(8,128)S(1)}, u32[]{:S(2)}, u32[]{:S(2)}) %collective-permute-start.3) | collective-permute-done | bytes 65568 | tf_op jit(solution)/shard_map/ppermute | solution.py:360
  23.5 0.5 %collective-permute-start.4 = (f32[2,32,512]{2,1,0:T(8,128)S(1)}, f32[2,32,512]{2,1,0:T(8,128)S(1)}, u32[]{:S(2)}, u32[]{:S(2)}) collective-permute-start(f32[2,32,512]{2,1,0:T(8,128)S(1)} %pad_maximum_fusion.5), channel_id=1, source_target_pairs={{0,1},{1,0},{2,3},{3,2},{4,5},{5,4},{6,7},{7,6},{8,9},{9,8},{10,11... | collective-permute-start | bytes 393224 | tf_op jit(solution)/shard_map/ppermute | solution.py:360
  24.1 0.0 collective-permute-done.5
  24.1 0.0 collective-permute-done.6
  24.2 6.2 %partial_sums.1 = f32[1,4096]{1,0:T(1,128)S(1)} custom-call(s32[8,128]{1,0:T(8,128)S(1)} %get-tuple-element.31.info_ref, s32[8,128]{1,0:T(8,128)S(1)} %slice.11.counts_ref, bf16[8,128,128]{2,1,0:T(8,128)(2,1)S(1)} %pad_maximum_fusion.2.a_ref, bf16[1792,128]{1,0:T(8,128)(2,1)S(1)} %pad_maximum_fusion.g_ref, f32[1792,128]{1,0:T(8,128)S(1)} %sign_table.1.after_too_ref.sign_ref, ...), custom_call_target="tpu_custom_call" | custom-call | flops 7000000000 | bytes 1000000 | tf_op jit(solution)/shard_map/partial_sums/pallas_call | solution.py:306
  30.4 0.1 collective-permute-start.7
  30.5 1.2 %collective-permute-done.7 = f32[1,4096]{1,0:T(1,128)S(1)} collective-permute-done((f32[1,4096]{1,0:T(1,128)S(1)}, f32[1,4096]{1,0:T(1,128)S(1)}, u32[]{:S(2)}, u32[]{:S(2)}) %collective-permute-start.7) | collective-permute-done | bytes 16416 | tf_op jit(solution)/shard_map/ppermute | solution.py:360
  31.7 0.0 collective-permute-done.4.q2_ref
  31.7 2.5 %collective-permute-start.12 = (f32[4,32,512]{2,1,0:T(8,128)S(1)}, f32[4,32,512]{2,1,0:T(8,128)S(1)}, u32[]{:S(2)}, u32[]{:S(2)}) collective-permute-start(f32[4,32,512]{2,1,0:T(8,128)S(1)} %pad_maximum_fusion.1), channel_id=1, source_target_pairs={{0,3},{1,2},{2,1},{3,0},{4,7},{5,6},{6,5},{7,4},{8,11},{9,10},{10,... | collective-permute-start | bytes 786440 | tf_op jit(solution)/shard_map/ppermute | solution.py:360
  34.2 0.6 %collective-permute-start.8 = (f32[1,4096]{1,0:T(1,128)S(1)}, f32[1,4096]{1,0:T(1,128)S(1)}, u32[]{:S(2)}, u32[]{:S(2)}) collective-permute-start(f32[1,4096]{1,0:T(1,128)S(1)} %add.14), channel_id=1, source_target_pairs={{0,16},{8,24},{16,0},{24,8},{32,48},{40,56},{48,32},{56,40},{64,80... | collective-permute-start | bytes 49160 | tf_op jit(solution)/shard_map/ppermute | solution.py:360
  34.8 3.1 %collective-permute-done.8 = f32[1,4096]{1,0:T(1,128)S(1)} collective-permute-done((f32[1,4096]{1,0:T(1,128)S(1)}, f32[1,4096]{1,0:T(1,128)S(1)}, u32[]{:S(2)}, u32[]{:S(2)}) %collective-permute-start.8) | collective-permute-done | bytes 16416 | tf_op jit(solution)/shard_map/ppermute | solution.py:360
  38.0 1.2 %collective-permute-start.9 = (f32[1,4096]{1,0:T(1,128)S(1)}, f32[1,4096]{1,0:T(1,128)S(1)}, u32[]{:S(2)}, u32[]{:S(2)}) collective-permute-start(f32[1,4096]{1,0:T(1,128)S(1)} %add.15), channel_id=1, source_target_pairs={{0,48},{8,56},{16,32},{24,40},{32,16},{40,24},{48,0},{56,8},{64,11... | collective-permute-start | bytes 49160 | tf_op jit(solution)/shard_map/ppermute | solution.py:360
  39.2 3.8 %collective-permute-done.9 = f32[1,4096]{1,0:T(1,128)S(1)} collective-permute-done((f32[1,4096]{1,0:T(1,128)S(1)}, f32[1,4096]{1,0:T(1,128)S(1)}, u32[]{:S(2)}, u32[]{:S(2)}) %collective-permute-start.9) | collective-permute-done | bytes 16416 | tf_op jit(solution)/shard_map/ppermute | solution.py:360
  43.0 1.3 %collective-permute-start.10 = (f32[1,4096]{1,0:T(1,128)S(1)}, f32[1,4096]{1,0:T(1,128)S(1)}, u32[]{:S(2)}, u32[]{:S(2)}) collective-permute-start(f32[1,4096]{1,0:T(1,128)S(1)} %add.16), channel_id=1, source_target_pairs={{0,64},{8,72},{16,80},{24,88},{32,96},{40,104},{48,112},{56,120},{... | collective-permute-start | bytes 49160 | tf_op jit(solution)/shard_map/ppermute | solution.py:360
  44.3 2.5 %collective-permute-done.10 = f32[1,4096]{1,0:T(1,128)S(1)} collective-permute-done((f32[1,4096]{1,0:T(1,128)S(1)}, f32[1,4096]{1,0:T(1,128)S(1)}, u32[]{:S(2)}, u32[]{:S(2)}) %collective-permute-start.10) | collective-permute-done | bytes 16416 | tf_op jit(solution)/shard_map/ppermute | solution.py:360
  46.9 2.6 %collective-permute-start.11 = (f32[1,4096]{1,0:T(1,128)S(1)}, f32[1,4096]{1,0:T(1,128)S(1)}, u32[]{:S(2)}, u32[]{:S(2)}) collective-permute-start(f32[1,4096]{1,0:T(1,128)S(1)} %add.17.mine_ref), channel_id=1, source_target_pairs={{0,128},{8,136},{16,144},{24,152},{32,160},{40,168},{48,176},{56,1... | collective-permute-start | bytes 49160 | tf_op jit(solution)/shard_map/ppermute | solution.py:360
  49.5 2.1 %collective-permute-done.11.other_ref = f32[1,4096]{1,0:T(1,128)S(1)} collective-permute-done((f32[1,4096]{1,0:T(1,128)S(1)}, f32[1,4096]{1,0:T(1,128)S(1)}, u32[]{:S(2)}, u32[]{:S(2)}) %collective-permute-start.11) | collective-permute-done | bytes 16416 | tf_op jit(solution)/shard_map/ppermute | solution.py:360
  51.6 0.0 collective-permute-done.12.q3_ref
  51.6 0.7 %finish.1 = (f32[1,4096]{1,0:T(1,128)}, f32[1,32]{1,0:T(1,128)}) custom-call(f32[1,4096]{1,0:T(1,128)S(1)} %add.17.mine_ref, f32[1,4096]{1,0:T(1,128)S(1)} %collective-permute-done.11.other_ref, f32[32,512]{1,0:T(8,128)S(1)} %copy-done, f32[1,32,512]{2,1,0:T(8,128)S(1)} %collective-permute-done.3.q1_ref, f32[2,32,512]{2,1,0:T(8,128)S(1)} %collective-permute-done.4.q2_ref, ...), custom_call_target="tpu_custom_call" | custom-call | flops 1000000000 | bytes 1000000 | tf_op jit(solution)/shard_map/finish/pallas_call | solution.py:344
  (16 shorter events, 0.2 us)
Async XLA Ops:
  0.6 10.2 %copy-start.1 = (s32[128,547]{0,1:T(8,128)S(1)}, s32[128,547]{0,1:T(8,128)}, u32[]{:S(2)}) copy-start(s32[128,547]{0,1:T(8,128)} %param.10) | copy-start | bytes 840196
  0.6 6.5 %collective-permute-start = (bf16[1,128,128]{2,1,0:T(8,128)(2,1)}, bf16[1,128,128]{2,1,0:T(8,128)(2,1)S(1)}, u32[]{:S(2)}, u32[]{:S(2)}) collective-permute-start(bf16[1,128,128]{2,1,0:T(8,128)(2,1)} %param.7), channel_id=1, source_target_pairs={{0,128},{8,136},{16,144},{24,152},{32,160},{40,168},{48,176},{56,1... | collective-permute-start | bytes 98312 | tf_op jit(solution)/shard_map/ppermute | solution.py:360
  4.0 3.1 %collective-permute-start.1 = (bf16[448,128]{1,0:T(8,128)(2,1)}, bf16[448,128]{1,0:T(8,128)(2,1)S(1)}, u32[]{:S(2)}, u32[]{:S(2)}) collective-permute-start(bf16[448,128]{1,0:T(8,128)(2,1)} %bitcast.15), channel_id=1, source_target_pairs={{0,8},{8,0},{16,24},{24,16},{32,40},{40,32},{48,56},{56,48},{64,72... | collective-permute-start | bytes 344072 | tf_op jit(solution)/shard_map/ppermute | solution.py:360
  7.2 5.8 %collective-permute-start.2 = (bf16[2,128,128]{2,1,0:T(8,128)(2,1)S(1)}, bf16[2,128,128]{2,1,0:T(8,128)(2,1)S(1)}, u32[]{:S(2)}, u32[]{:S(2)}) collective-permute-start(bf16[2,128,128]{2,1,0:T(8,128)(2,1)S(1)} %pad_maximum_fusion.6), channel_id=1, source_target_pairs={{0,64},{8,72},{16,80},{24,88},{32,96},{40,104},{48,112},{56,120},{... | collective-permute-start | bytes 196616 | tf_op jit(solution)/shard_map/ppermute | solution.py:360
  9.2 14.9 %collective-permute-start.6 = (bf16[896,128]{1,0:T(8,128)(2,1)S(1)}, bf16[896,128]{1,0:T(8,128)(2,1)S(1)}, u32[]{:S(2)}, u32[]{:S(2)}) collective-permute-start(bf16[896,128]{1,0:T(8,128)(2,1)S(1)} %pad_maximum_fusion.3.after_ref), channel_id=1, source_target_pairs={{0,16},{8,24},{16,0},{24,8},{32,48},{40,56},{48,32},{56,40},{64,80... | collective-permute-start | bytes 688136 | tf_op jit(solution)/shard_map/ppermute | solution.py:360
  11.5 3.8 %copy-start = (f32[32,512]{1,0:T(8,128)S(1)}, f32[32,512]{1,0:T(8,128)}, u32[]{:S(2)}) copy-start(f32[32,512]{1,0:T(8,128)} %q0_ref.1) | copy-start | bytes 196612
  13.1 11.0 %collective-permute-start.5 = (bf16[4,128,128]{2,1,0:T(8,128)(2,1)S(1)}, bf16[4,128,128]{2,1,0:T(8,128)(2,1)S(1)}, u32[]{:S(2)}, u32[]{:S(2)}) collective-permute-start(bf16[4,128,128]{2,1,0:T(8,128)(2,1)S(1)} %constant_dynamic-update-slice_fusion.after_ref), channel_id=1, source_target_pairs={{0,48},{8,56},{16,32},{24,40},{32,16},{40,24},{48,0},{56,8},{64,11... | collective-permute-start | bytes 393224 | tf_op jit(solution)/shard_map/ppermute | solution.py:360
  15.3 8.3 %collective-permute-start.3 = (f32[1,32,512]{2,1,0:T(8,128)S(1)}, f32[1,32,512]{2,1,0:T(8,128)S(1)}, u32[]{:S(2)}, u32[]{:S(2)}) collective-permute-start(f32[1,32,512]{2,1,0:T(8,128)S(1)} %bitcast.12), channel_id=1, source_target_pairs={{0,4},{1,5},{2,6},{3,7},{4,0},{5,1},{6,2},{7,3},{8,12},{9,13},{10,... | collective-permute-start | bytes 196616 | tf_op jit(solution)/shard_map/ppermute | solution.py:360
  23.5 8.2 %collective-permute-start.4 = (f32[2,32,512]{2,1,0:T(8,128)S(1)}, f32[2,32,512]{2,1,0:T(8,128)S(1)}, u32[]{:S(2)}, u32[]{:S(2)}) collective-permute-start(f32[2,32,512]{2,1,0:T(8,128)S(1)} %pad_maximum_fusion.5), channel_id=1, source_target_pairs={{0,1},{1,0},{2,3},{3,2},{4,5},{5,4},{6,7},{7,6},{8,9},{9,8},{10,11... | collective-permute-start | bytes 393224 | tf_op jit(solution)/shard_map/ppermute | solution.py:360
  30.4 1.3 %collective-permute-start.7 = (f32[1,4096]{1,0:T(1,128)S(1)}, f32[1,4096]{1,0:T(1,128)S(1)}, u32[]{:S(2)}, u32[]{:S(2)}) collective-permute-start(f32[1,4096]{1,0:T(1,128)S(1)} %partial_sums.1), channel_id=1, source_target_pairs={{0,8},{8,0},{16,24},{24,16},{32,40},{40,32},{48,56},{56,48},{64,72... | collective-permute-start | bytes 49160 | tf_op jit(solution)/shard_map/ppermute | solution.py:360
  31.7 19.9 %collective-permute-start.12 = (f32[4,32,512]{2,1,0:T(8,128)S(1)}, f32[4,32,512]{2,1,0:T(8,128)S(1)}, u32[]{:S(2)}, u32[]{:S(2)}) collective-permute-start(f32[4,32,512]{2,1,0:T(8,128)S(1)} %pad_maximum_fusion.1), channel_id=1, source_target_pairs={{0,3},{1,2},{2,1},{3,0},{4,7},{5,6},{6,5},{7,4},{8,11},{9,10},{10,... | collective-permute-start | bytes 786440 | tf_op jit(solution)/shard_map/ppermute | solution.py:360
  34.2 3.7 %collective-permute-start.8 = (f32[1,4096]{1,0:T(1,128)S(1)}, f32[1,4096]{1,0:T(1,128)S(1)}, u32[]{:S(2)}, u32[]{:S(2)}) collective-permute-start(f32[1,4096]{1,0:T(1,128)S(1)} %add.14), channel_id=1, source_target_pairs={{0,16},{8,24},{16,0},{24,8},{32,48},{40,56},{48,32},{56,40},{64,80... | collective-permute-start | bytes 49160 | tf_op jit(solution)/shard_map/ppermute | solution.py:360
  38.0 5.0 %collective-permute-start.9 = (f32[1,4096]{1,0:T(1,128)S(1)}, f32[1,4096]{1,0:T(1,128)S(1)}, u32[]{:S(2)}, u32[]{:S(2)}) collective-permute-start(f32[1,4096]{1,0:T(1,128)S(1)} %add.15), channel_id=1, source_target_pairs={{0,48},{8,56},{16,32},{24,40},{32,16},{40,24},{48,0},{56,8},{64,11... | collective-permute-start | bytes 49160 | tf_op jit(solution)/shard_map/ppermute | solution.py:360
  43.0 3.8 %collective-permute-start.10 = (f32[1,4096]{1,0:T(1,128)S(1)}, f32[1,4096]{1,0:T(1,128)S(1)}, u32[]{:S(2)}, u32[]{:S(2)}) collective-permute-start(f32[1,4096]{1,0:T(1,128)S(1)} %add.16), channel_id=1, source_target_pairs={{0,64},{8,72},{16,80},{24,88},{32,96},{40,104},{48,112},{56,120},{... | collective-permute-start | bytes 49160 | tf_op jit(solution)/shard_map/ppermute | solution.py:360
  46.9 4.7 %collective-permute-start.11 = (f32[1,4096]{1,0:T(1,128)S(1)}, f32[1,4096]{1,0:T(1,128)S(1)}, u32[]{:S(2)}, u32[]{:S(2)}) collective-permute-start(f32[1,4096]{1,0:T(1,128)S(1)} %add.17.mine_ref), channel_id=1, source_target_pairs={{0,128},{8,136},{16,144},{24,152},{32,160},{40,168},{48,176},{56,1... | collective-permute-start | bytes 49160 | tf_op jit(solution)/shard_map/ppermute | solution.py:360

commit v3 on v2

--- a/solution.py
+++ b/solution.py
@@ -18,12 +18,13 @@
 GROUPS = ROW_GROUPS * COL_GROUPS
 BLK = 128
 MAXB = 96
-UNROLL = 16
+UNROLL = 32
 PIECES = 4
 RUNS_HERE = PIECES * RUNS
 
 ROW_STEPS = (16, 8, 6)
-COL_STEPS = (1, 2)
+COL_STEPS = (2, 1)
+PIECE = (0, 2, 1, 3)
 SUM_STEPS = (1, 2, 6, 8, 16)
 EX_STEPS = (4, 1, 3)
 
@@ -149,49 +150,22 @@
     )(coord, place, after, after_too)
 
 
-def coord_signs_kernel(info_ref, sorted_ref, after_ref, u_ref, vl_ref, vj_ref):
-    feat = lax.axis_index("feat")
-    run = iota((32, BLK), 0)
-    piece = (run * 37) >> 8
-    run = RUNS * (feat ^ piece) + (run - RUNS * piece)
+def block_signs(sorted_ref, b, run, feat):
+    row = sorted_ref[pl.ds(b, 1), :]
+    col_high = sorted_ref[pl.ds(MAXB + b, 1), :]
+    rest = sorted_ref[pl.ds(2 * MAXB + b, 1), :]
     eight = iota((8, BLK), 0)
-
-    def step(i, carry):
-        for n in range(UNROLL):
-            b = i * UNROLL + n
-            row = sorted_ref[pl.ds(b, 1), :]
-            col_high = sorted_ref[pl.ds(MAXB + b, 1), :]
-            rest = sorted_ref[pl.ds(2 * MAXB + b, 1), :]
-            column = [sign_of(parity3(eight & row))]
-            for bit in range(3, 7):
-                turn = sign_of((row >> bit) & 1)
-                column = column + [part * turn for part in column]
-            u_ref[b] = jnp.concatenate(column, axis=0).astype(BF16)
-            flip = parity((rest >> 3) & feat)
-            vl_ref[b] = sign_of(parity3(eight & rest) ^ flip) * (1.0 / math.sqrt(DIN * DPAD))
-            vj_ref[b] = sign_of(parity(run & col_high))
-        return carry
-
-    lax.fori_loop(0, (info_ref[1, 0] + (UNROLL - 1)) // UNROLL, step, 0)
-
-
-def coord_signs(info, sorted_fields, after):
-    return pl.pallas_call(
-        coord_signs_kernel,
-        out_shape=(
-            jax.ShapeDtypeStruct((MAXB, 128, BLK), BF16),
-            jax.ShapeDtypeStruct((MAXB, 8, BLK), F32),
-            jax.ShapeDtypeStruct((MAXB, 32, BLK), F32),
-        ),
-        in_specs=[
-            pl.BlockSpec(memory_space=pltpu.SMEM),
-            pl.BlockSpec(memory_space=pltpu.VMEM),
-            pl.BlockSpec(memory_space=pl.ANY),
-        ],
-        compiler_params=pltpu.CompilerParams(vmem_limit_bytes=8 * 2**20),
-        cost_estimate=cost(3),
-        name="coord_signs",
-    )(info, sorted_fields, after)
+    column = [sign_of(parity3(eight & row))]
+    for bit in range(3, 7):
+        turn = sign_of((row >> bit) & 1)
+        column = column + [part * turn for part in column]
+    flip = parity((rest >> 3) & feat)
+    scale = 1.0 / math.sqrt(DIN * DPAD)
+    return (
+        jnp.concatenate(column, axis=0).astype(BF16),
+        sign_of(parity3(eight & rest) ^ flip) * scale,
+        sign_of(parity(run & col_high)),
+    )
 
 
 def table_kernel(words_ref, after_ref, sign_ref):
@@ -202,7 +176,7 @@
         [((words >> (8 * p)) & 255).astype(F32) for p in range(4)], axis=0
     ).astype(BF16)
     for e in range(PIECES):
-        col = COLS * (feat ^ e) + iota((COLS, 128), 0)
+        col = COLS * (feat ^ PIECE[e]) + iota((COLS, 128), 0)
         word = (col * 34953) >> 20
         bit = col - 30 * word
         target = ((bit >> 3) << 6) + (word - first_word)
@@ -241,7 +215,7 @@
 
 
 def main_kernel(
-    info_ref, counts_ref, a_ref, g_ref, sign_ref, u_ref, vl_ref, vj_ref, low_ref, high_ref,
+    info_ref, counts_ref, a_ref, g_ref, sign_ref, sorted_ref, low_ref, high_ref,
     out_ref, mixed_ref, signed_ref, block_ref,
 ):
     for first in range(0, TOK, 32):
@@ -280,16 +254,21 @@
                         signed_ref[group + h, to : to + 16, 0:128] = high
                         signed_ref[group + h, to : to + 16, 128:256] = low
     block_ref[...] = jnp.zeros_like(block_ref)
+    feat = lax.axis_index("feat")
+    run = iota((32, BLK), 0)
+    piece = (run * 37) >> 8
+    run = RUNS * (feat ^ ((piece & 1) << 1) ^ (piece >> 1)) + (run - RUNS * piece)
 
     def step(i, carry):
         for n in range(UNROLL):
             b = i * UNROLL + n
-            weights = jnp.concatenate([u_ref[b], u_ref[b]], axis=0)
+            column, low_signs, run_signs = block_signs(sorted_ref, b, run, feat)
+            weights = jnp.concatenate([column, column], axis=0)
             rows = jnp.dot(signed_ref[info_ref[0, b]], weights, preferred_element_type=F32)
-            total = vj_ref[b, 0:1, :] * rows[0:8]
+            total = run_signs[0:1] * rows[0:8]
             for j in range(1, RUNS_HERE):
-                total = total + vj_ref[b, j : j + 1, :] * rows[8 * j : 8 * j + 8]
-            block_ref[pl.ds(b, 1), :] = jnp.sum(total * vl_ref[b], axis=0, keepdims=True)
+                total = total + run_signs[j : j + 1] * rows[8 * j : 8 * j + 8]
+            block_ref[pl.ds(b, 1), :] = jnp.sum(total * low_signs, axis=0, keepdims=True)
         return carry
 
     lax.fori_loop(0, (info_ref[1, 0] + (UNROLL - 1)) // UNROLL, step, 0)
@@ -301,12 +280,12 @@
         out_ref[:, at] = jnp.sum(spread * high_ref[:, at].astype(F32), axis=0, keepdims=True)
 
 
-def partial_sums(info, counts, acts, grads, signs, u, vl, vj, low, high):
+def partial_sums(info, counts, acts, grads, signs, sorted_fields, low, high):
     vmem = pl.BlockSpec(memory_space=pltpu.VMEM)
     return pl.pallas_call(
         main_kernel,
         out_shape=jax.ShapeDtypeStruct((1, PROJ), F32),
-        in_specs=[pl.BlockSpec(memory_space=pltpu.SMEM)] + [vmem] * 9,
+        in_specs=[pl.BlockSpec(memory_space=pltpu.SMEM)] + [vmem] * 7,
         out_specs=vmem,
         scratch_shapes=[
             pltpu.VMEM((2 * TOK, ROW_GROUPS * 128), BF16),
@@ -316,7 +295,7 @@
         cost_estimate=cost(7),
         compiler_params=pltpu.CompilerParams(vmem_limit_bytes=16 * 2**20),
         name="partial_sums",
-    )(info, counts, acts, grads, signs, u, vl, vj, low, high)
+    )(info, counts, acts, grads, signs, sorted_fields, low, high)
 
 
 def finish_kernel(mine_ref, other_ref, q0_ref, q1_ref, q2_ref, q3_ref, proj_ref, score_ref, row_ref):
@@ -356,6 +335,27 @@
     )(mine, other, *queries)
 
 
+def join_kernel(*refs):
+    parts, out_ref = refs[:-2], refs[-1]
+    rows = out_ref.shape[0] // len(parts)
+    for n, ref in enumerate(parts):
+        out_ref[rows * n : rows * n + rows] = ref[...]
+
+
+def join(parts, after):
+    vmem = pl.BlockSpec(memory_space=pltpu.VMEM)
+    shape = (len(parts) * parts[0].shape[0],) + parts[0].shape[1:]
+    return pl.pallas_call(
+        join_kernel,
+        out_shape=jax.ShapeDtypeStruct(shape, parts[0].dtype),
+        in_specs=[vmem] * len(parts) + [pl.BlockSpec(memory_space=pl.ANY)],
+        out_specs=vmem,
+        compiler_params=pltpu.CompilerParams(vmem_limit_bytes=2**20),
+        cost_estimate=cost(1),
+        name="join",
+    )(*parts, after)
+
+
 def swap(value, axis, size, step):
     return lax.ppermute(value, axis, [(i, i ^ step) for i in range(size)])
 
@@ -370,31 +370,26 @@
     ).reshape(40, 128)
     own, ints = lax.optimization_barrier((own, ints))
     place, info = rank_coords(ints, own)
-    own, got, got_grads, _ = lax.optimization_barrier((own, got, got_grads, place))
+    own, got, _ = lax.optimization_barrier((own, got, place))
     acts = jnp.concatenate([own[None, :TOK], got], axis=0)
     grads = jnp.concatenate([own[TOK:], got_grads], axis=0)
     got = swap(acts, "feat", 32, ROW_STEPS[1])
     got_grads = swap(grads, "feat", 32, COL_STEPS[1])
-    signs = sign_table(sign_words.T, grads)
-    sorted_fields, low, high = sort_coords(ints, place, grads, signs)
+    signs = sign_table(sign_words.T, acts)
+    sorted_fields, low, high = sort_coords(ints, place, acts, signs)
     acts, got, _ = lax.optimization_barrier((acts, got, sorted_fields))
     acts = jnp.concatenate([acts, got], axis=0)
     got = swap(acts, "feat", 32, ROW_STEPS[2])
-    u, vl, vj = coord_signs(info, sorted_fields, acts)
-    q, _ = lax.optimization_barrier((queries[None], acts))
+    q = join([queries[None]], acts)
     got_q = [swap(q, "ex", 8, EX_STEPS[0])]
-    q = jnp.concatenate([q, got_q[-1]], axis=0)
-    q, _ = lax.optimization_barrier((q, u))
-    got_q.append(swap(q, "ex", 8, EX_STEPS[1]))
-    q = jnp.concatenate([q, got_q[-1]], axis=0)
     acts = jnp.concatenate([acts, got], axis=0)
     grads = jnp.concatenate([grads, got_grads], axis=0)
-    total = partial_sums(info, ints[32:], acts, grads, signs, u, vl, vj, low, high)
+    total = partial_sums(info, ints[32:], acts, grads, signs, sorted_fields, low, high)
     for n, step in enumerate(SUM_STEPS[:-1]):
         total = total + swap(total, "feat", 32, step)
-        if n == 0:
-            q, total = lax.optimization_barrier((q, total))
-            got_q.append(swap(q, "ex", 8, EX_STEPS[2]))
+        if n in (0, 2):
+            q, total = lax.optimization_barrier((jnp.concatenate([q, got_q[-1]], axis=0), total))
+            got_q.append(swap(q, "ex", 8, EX_STEPS[len(got_q)]))
     other = swap(total, "feat", 32, SUM_STEPS[-1])
     return finish(total, other, [queries] + got_q)
 

time: 52.8 us -> 49 us (0.928)
  Pallas kernels: 11.6 us -> 9.67 us
  starting transfers between devices: 22.9 us -> 22.1 us
  other arithmetic: 1.85 us -> 1.12 us
    pallas_call x1, Pallas kernels: 1.67 us -> 0.01 us  [join(): pl.pallas_call(join_kernel, out_shape=jax.ShapeDtypeStruct(shape, parts[0...]
    ppermute x13, starting transfers between devices: 22.9 us -> 22.1 us  [swap(): return lax.ppermute(value, axis, [(i, i ^ step) for i in range(size)])]
    or x1, other arithmetic: 0.74 us -> 0.01 us  [body(): coord_row << 14 | coord_col]
  transfers between devices with their start and end apart: 13 -> 13, of which waited for: 6 -> 6; matrix products, arithmetic and copies ran while one was open for 4% -> 2% of each run, Pallas kernels for 21% -> 18%
where the time goes in v3:
time: 49 us; the launch traced here: 48.9 us
  starting transfers between devices  22.1 us (45%)
  waiting for transfers between devices  14.5 us (30%)
  Pallas kernels  9.67 us (20%)
  between operations  1.5 us (3%)
  other arithmetic  1.12 us (2%)
    ppermute x13, starting transfers between devices, swap(): return lax.ppermute(value, axis, [(i, i ^ step) for i in range(size)])  22.1 us
    ppermute x13, waiting for transfers between devices, swap(): return lax.ppermute(value, axis, [(i, i ^ step) for i in range(size)])  14.5 us
    pallas_call x1, Pallas kernels, partial_sums(): pl.pallas_call(main_kernel, out_shape=jax.ShapeDtypeStruct((1, PROJ), F32...  5.97 us
    pallas_call x1, Pallas kernels, sort_coords(): pl.pallas_call(sort_kernel, out_shape=(jax.ShapeDtypeStruct((3 * MAXB, BL...  1.55 us
  transfers between devices with their start and end apart: 13, of which 6 were waited for; matrix products, arithmetic and copies ran while one was open for 2% of the time, Pallas kernels for 18%

profile of v3, /device:TPU:8, one launch (start us, length us, event | category | flops | bytes accessed | tf_op | source)
XLA Modules:
  0.0 48.9 jit_solution(18005103480228138038)
XLA Ops:
  0.6 3.4 %collective-permute-start = (bf16[1,128,128]{2,1,0:T(8,128)(2,1)}, bf16[1,128,128]{2,1,0:T(8,128)(2,1)S(1)}, u32[]{:S(2)}, u32[]{:S(2)}) collective-permute-start(bf16[1,128,128]{2,1,0:T(8,128)(2,1)} %param.7), channel_id=1, source_target_pairs={{0,128},{8,136},{16,144},{24,152},{32,160},{40,168},{48,176},{56,1... | collective-permute-start | bytes 98312 | tf_op jit(solution)/shard_map/ppermute | solution.py:360
  4.0 1.5 %collective-permute-start.4 = (bf16[448,128]{1,0:T(8,128)(2,1)}, bf16[448,128]{1,0:T(8,128)(2,1)S(1)}, u32[]{:S(2)}, u32[]{:S(2)}) collective-permute-start(bf16[448,128]{1,0:T(8,128)(2,1)} %bitcast.14), channel_id=1, source_target_pairs={{0,16},{8,24},{16,0},{24,8},{32,48},{40,56},{48,32},{56,40},{64,80... | collective-permute-start | bytes 344072 | tf_op jit(solution)/shard_map/ppermute | solution.py:360
  6.1 0.0 copy-start.2
  6.1 0.0 copy-start.3
  6.2 0.9 %pad_maximum_fusion.4.after_ref = bf16[576,128]{1,0:T(8,128)(2,1)S(1)} fusion(bf16[448,128]{1,0:T(8,128)(2,1)} %bitcast.15, bf16[128,128]{1,0:T(8,128)(2,1)} %bitcast.16), kind=kLoop, calls=%fused_computation.4 | loop fusion | flops 294912 | bytes 294912 | tf_op jit(solution)/shard_map/concatenate | solution.py:367
  7.1 0.0 copy-done.2
  7.1 0.0 copy-done.3
  7.1 0.0 copy-start
  7.1 0.8 %rank_coords.1 = (s32[32,128]{1,0:T(8,128)S(1)}, s32[8,128]{1,0:T(8,128)S(1)}) custom-call(s32[40,128]{1,0:T(8,128)S(1)} %pad_bitcast_fusion.ints_ref.coord_ref, bf16[576,128]{1,0:T(8,128)(2,1)S(1)} %pad_maximum_fusion.4.after_ref), custom_call_target="tpu_custom_call" | custom-call | flops 1000000000 | bytes 1000000 | tf_op jit(solution)/shard_map/rank_coords/pallas_call | solution.py:102
  7.9 0.0 collective-permute-done
  8.0 2.0 %collective-permute-start.1 = (bf16[2,128,128]{2,1,0:T(8,128)(2,1)S(1)}, bf16[2,128,128]{2,1,0:T(8,128)(2,1)S(1)}, u32[]{:S(2)}, u32[]{:S(2)}) collective-permute-start(bf16[2,128,128]{2,1,0:T(8,128)(2,1)S(1)} %pad_maximum_fusion.6.after_ref), channel_id=1, source_target_pairs={{0,64},{8,72},{16,80},{24,88},{32,96},{40,104},{48,112},{56,120},{... | collective-permute-start | bytes 196616 | tf_op jit(solution)/shard_map/ppermute | solution.py:360
  10.0 0.0 copy-done
  10.0 0.7 %sign_table.1.after_too_ref.sign_ref = f32[1792,128]{1,0:T(8,128)S(1)} custom-call(s32[547,128]{1,0:T(8,128)S(1)} %bitcast.12, bf16[2,128,128]{2,1,0:T(8,128)(2,1)S(1)} %pad_maximum_fusion.6.after_ref), custom_call_target="tpu_custom_call" | custom-call | flops 2000000000 | bytes 1000000 | tf_op jit(solution)/shard_map/sign_table/pallas_call | solution.py:192
  10.6 1.5 %sort_coords.1 = (s32[288,128]{1,0:T(8,128)S(1)}, bf16[128,4096]{1,0:T(8,128)(2,1)S(1)}, bf16[96,4096]{1,0:T(8,128)(2,1)S(1)}) custom-call(s32[40,128]{1,0:T(8,128)S(1)} %pad_bitcast_fusion.ints_ref.coord_ref, s32[32,128]{1,0:T(8,128)S(1)} %get-tuple-element.19.place_ref, bf16[2,128,128]{2,1,0:T(8,128)(2,1)S(1)} %pad_maximum_fusion.6.after_ref, ...), custom_call_target="tpu_custom_call" | custom-call | flops 2000000000 | bytes 1000000 | tf_op jit(solution)/shard_map/sort_coords/pallas_call | solution.py:138
  12.2 0.1 collective-permute-done.1
  12.3 0.0 copy-start.1
  12.3 2.2 %collective-permute-start.3 = (bf16[4,128,128]{2,1,0:T(8,128)(2,1)S(1)}, bf16[4,128,128]{2,1,0:T(8,128)(2,1)S(1)}, u32[]{:S(2)}, u32[]{:S(2)}) collective-permute-start(bf16[4,128,128]{2,1,0:T(8,128)(2,1)S(1)} %constant_dynamic-update-slice_fusion.refs_1_), channel_id=1, source_target_pairs={{0,48},{8,56},{16,32},{24,40},{32,16},{40,24},{48,0},{56,8},{64,11... | collective-permute-start | bytes 393224 | tf_op jit(solution)/shard_map/ppermute | solution.py:360
  14.5 0.0 collective-permute-done.4
  14.6 0.1 collective-permute-start.5
  14.7 0.0 copy-done.1
  14.7 5.7 %collective-permute-start.2 = (f32[1,32,512]{2,1,0:T(8,128)S(1)}, f32[1,32,512]{2,1,0:T(8,128)S(1)}, u32[]{:S(2)}, u32[]{:S(2)}) collective-permute-start(f32[1,32,512]{2,1,0:T(8,128)S(1)} %join.1), channel_id=1, source_target_pairs={{0,4},{1,5},{2,6},{3,7},{4,0},{5,1},{6,2},{7,3},{8,12},{9,13},{10,... | collective-permute-start | bytes 196616 | tf_op jit(solution)/shard_map/ppermute | solution.py:360
  20.4 0.0 collective-permute-done.3
  20.5 0.0 collective-permute-done.5
  20.5 6.0 %partial_sums.1 = f32[1,4096]{1,0:T(1,128)S(1)} custom-call(s32[8,128]{1,0:T(8,128)S(1)} %get-tuple-element.25.info_ref, s32[8,128]{1,0:T(8,128)S(1)} %slice.10.counts_ref, bf16[8,128,128]{2,1,0:T(8,128)(2,1)S(1)} %pad_maximum_fusion.1.a_ref, bf16[1792,128]{1,0:T(8,128)(2,1)S(1)} %pad_maximum_fusion.g_ref, f32[1792,128]{1,0:T(8,128)S(1)} %sign_table.1.after_too_ref.sign_ref, ...), custom_call_target="tpu_custom_call" | custom-call | flops 7000000000 | bytes 1000000 | tf_op jit(solution)/shard_map/partial_sums/pallas_call | solution.py:285
  26.5 0.3 collective-permute-start.6
  26.8 0.0 collective-permute-done.2.q1_ref
  26.8 1.0 %collective-permute-done.6 = f32[1,4096]{1,0:T(1,128)S(1)} collective-permute-done((f32[1,4096]{1,0:T(1,128)S(1)}, f32[1,4096]{1,0:T(1,128)S(1)}, u32[]{:S(2)}, u32[]{:S(2)}) %collective-permute-start.6) | collective-permute-done | bytes 16416 | tf_op jit(solution)/shard_map/ppermute | solution.py:360
  27.8 0.5 %collective-permute-start.7 = (f32[2,32,512]{2,1,0:T(8,128)S(1)}, f32[2,32,512]{2,1,0:T(8,128)S(1)}, u32[]{:S(2)}, u32[]{:S(2)}) collective-permute-start(f32[2,32,512]{2,1,0:T(8,128)S(1)} %pad_maximum_fusion.5), channel_id=1, source_target_pairs={{0,1},{1,0},{2,3},{3,2},{4,5},{5,4},{6,7},{7,6},{8,9},{9,8},{10,11... | collective-permute-start | bytes 393224 | tf_op jit(solution)/shard_map/ppermute | solution.py:360
  28.3 0.3 collective-permute-start.8
  28.7 3.4 %collective-permute-done.8 = f32[1,4096]{1,0:T(1,128)S(1)} collective-permute-done((f32[1,4096]{1,0:T(1,128)S(1)}, f32[1,4096]{1,0:T(1,128)S(1)}, u32[]{:S(2)}, u32[]{:S(2)}) %collective-permute-start.8) | collective-permute-done | bytes 16416 | tf_op jit(solution)/shard_map/ppermute | solution.py:360
  32.1 1.0 %collective-permute-start.9 = (f32[1,4096]{1,0:T(1,128)S(1)}, f32[1,4096]{1,0:T(1,128)S(1)}, u32[]{:S(2)}, u32[]{:S(2)}) collective-permute-start(f32[1,4096]{1,0:T(1,128)S(1)} %add.15), channel_id=1, source_target_pairs={{0,48},{8,56},{16,32},{24,40},{32,16},{40,24},{48,0},{56,8},{64,11... | collective-permute-start | bytes 49160 | tf_op jit(solution)/shard_map/ppermute | solution.py:360
  33.0 4.1 %collective-permute-done.9 = f32[1,4096]{1,0:T(1,128)S(1)} collective-permute-done((f32[1,4096]{1,0:T(1,128)S(1)}, f32[1,4096]{1,0:T(1,128)S(1)}, u32[]{:S(2)}, u32[]{:S(2)}) %collective-permute-start.9) | collective-permute-done | bytes 16416 | tf_op jit(solution)/shard_map/ppermute | solution.py:360
  37.1 0.0 collective-permute-done.7.q2_ref
  37.2 2.5 %collective-permute-start.12 = (f32[4,32,512]{2,1,0:T(8,128)S(1)}, f32[4,32,512]{2,1,0:T(8,128)S(1)}, u32[]{:S(2)}, u32[]{:S(2)}) collective-permute-start(f32[4,32,512]{2,1,0:T(8,128)S(1)} %pad_maximum_fusion.2), channel_id=1, source_target_pairs={{0,3},{1,2},{2,1},{3,0},{4,7},{5,6},{6,5},{7,4},{8,11},{9,10},{10,... | collective-permute-start | bytes 786440 | tf_op jit(solution)/shard_map/ppermute | solution.py:360
  39.7 1.0 %collective-permute-start.10 = (f32[1,4096]{1,0:T(1,128)S(1)}, f32[1,4096]{1,0:T(1,128)S(1)}, u32[]{:S(2)}, u32[]{:S(2)}) collective-permute-start(f32[1,4096]{1,0:T(1,128)S(1)} %add.16), channel_id=1, source_target_pairs={{0,64},{8,72},{16,80},{24,88},{32,96},{40,104},{48,112},{56,120},{... | collective-permute-start | bytes 49160 | tf_op jit(solution)/shard_map/ppermute | solution.py:360
  40.7 2.7 %collective-permute-done.10 = f32[1,4096]{1,0:T(1,128)S(1)} collective-permute-done((f32[1,4096]{1,0:T(1,128)S(1)}, f32[1,4096]{1,0:T(1,128)S(1)}, u32[]{:S(2)}, u32[]{:S(2)}) %collective-permute-start.10) | collective-permute-done | bytes 16416 | tf_op jit(solution)/shard_map/ppermute | solution.py:360
  43.4 1.6 %collective-permute-start.11 = (f32[1,4096]{1,0:T(1,128)S(1)}, f32[1,4096]{1,0:T(1,128)S(1)}, u32[]{:S(2)}, u32[]{:S(2)}) collective-permute-start(f32[1,4096]{1,0:T(1,128)S(1)} %add.17.mine_ref), channel_id=1, source_target_pairs={{0,128},{8,136},{16,144},{24,152},{32,160},{40,168},{48,176},{56,1... | collective-permute-start | bytes 49160 | tf_op jit(solution)/shard_map/ppermute | solution.py:360
  45.0 3.2 %collective-permute-done.11.other_ref = f32[1,4096]{1,0:T(1,128)S(1)} collective-permute-done((f32[1,4096]{1,0:T(1,128)S(1)}, f32[1,4096]{1,0:T(1,128)S(1)}, u32[]{:S(2)}, u32[]{:S(2)}) %collective-permute-start.11) | collective-permute-done | bytes 16416 | tf_op jit(solution)/shard_map/ppermute | solution.py:360
  48.2 0.0 collective-permute-done.12.q3_ref
  48.2 0.7 %finish.1 = (f32[1,4096]{1,0:T(1,128)}, f32[1,32]{1,0:T(1,128)}) custom-call(f32[1,4096]{1,0:T(1,128)S(1)} %add.17.mine_ref, f32[1,4096]{1,0:T(1,128)S(1)} %collective-permute-done.11.other_ref, f32[32,512]{1,0:T(8,128)S(1)} %copy-done.1, f32[1,32,512]{2,1,0:T(8,128)S(1)} %collective-permute-done.2.q1_ref, f32[2,32,512]{2,1,0:T(8,128)S(1)} %collective-permute-done.7.q2_ref, ...), custom_call_target="tpu_custom_call" | custom-call | flops 1000000000 | bytes 1000000 | tf_op jit(solution)/shard_map/finish/pallas_call | solution.py:323
  (18 shorter events, 0.2 us)
Async XLA Ops:
  0.6 7.3 %collective-permute-start = (bf16[1,128,128]{2,1,0:T(8,128)(2,1)}, bf16[1,128,128]{2,1,0:T(8,128)(2,1)S(1)}, u32[]{:S(2)}, u32[]{:S(2)}) collective-permute-start(bf16[1,128,128]{2,1,0:T(8,128)(2,1)} %param.7), channel_id=1, source_target_pairs={{0,128},{8,136},{16,144},{24,152},{32,160},{40,168},{48,176},{56,1... | collective-permute-start | bytes 98312 | tf_op jit(solution)/shard_map/ppermute | solution.py:360
  4.0 10.5 %collective-permute-start.4 = (bf16[448,128]{1,0:T(8,128)(2,1)}, bf16[448,128]{1,0:T(8,128)(2,1)S(1)}, u32[]{:S(2)}, u32[]{:S(2)}) collective-permute-start(bf16[448,128]{1,0:T(8,128)(2,1)} %bitcast.14), channel_id=1, source_target_pairs={{0,16},{8,24},{16,0},{24,8},{32,48},{40,56},{48,32},{56,40},{64,80... | collective-permute-start | bytes 344072 | tf_op jit(solution)/shard_map/ppermute | solution.py:360
  6.1 0.9 %copy-start.2 = (s32[4096]{0:T(1024)S(1)}, s32[4096]{0:T(1024)}, u32[]{:S(2)}) copy-start(s32[4096]{0:T(1024)} %param.12) | copy-start | bytes 49156
  6.1 0.9 %copy-start.3 = (s32[4096]{0:T(1024)S(1)}, s32[4096]{0:T(1024)}, u32[]{:S(2)}) copy-start(s32[4096]{0:T(1024)} %param.11) | copy-start | bytes 49156
  7.1 2.8 %copy-start = (s32[128,547]{0,1:T(8,128)S(1)}, s32[128,547]{0,1:T(8,128)}, u32[]{:S(2)}) copy-start(s32[128,547]{0,1:T(8,128)} %param.10) | copy-start | bytes 840196
  8.0 4.4 %collective-permute-start.1 = (bf16[2,128,128]{2,1,0:T(8,128)(2,1)S(1)}, bf16[2,128,128]{2,1,0:T(8,128)(2,1)S(1)}, u32[]{:S(2)}, u32[]{:S(2)}) collective-permute-start(bf16[2,128,128]{2,1,0:T(8,128)(2,1)S(1)} %pad_maximum_fusion.6.after_ref), channel_id=1, source_target_pairs={{0,64},{8,72},{16,80},{24,88},{32,96},{40,104},{48,112},{56,120},{... | collective-permute-start | bytes 196616 | tf_op jit(solution)/shard_map/ppermute | solution.py:360
  12.3 2.3 %copy-start.1 = (f32[32,512]{1,0:T(8,128)S(1)}, f32[32,512]{1,0:T(8,128)}, u32[]{:S(2)}) copy-start(f32[32,512]{1,0:T(8,128)} %q0_ref.1) | copy-start | bytes 196612
  12.3 8.1 %collective-permute-start.3 = (bf16[4,128,128]{2,1,0:T(8,128)(2,1)S(1)}, bf16[4,128,128]{2,1,0:T(8,128)(2,1)S(1)}, u32[]{:S(2)}, u32[]{:S(2)}) collective-permute-start(bf16[4,128,128]{2,1,0:T(8,128)(2,1)S(1)} %constant_dynamic-update-slice_fusion.refs_1_), channel_id=1, source_target_pairs={{0,48},{8,56},{16,32},{24,40},{32,16},{40,24},{48,0},{56,8},{64,11... | collective-permute-start | bytes 393224 | tf_op jit(solution)/shard_map/ppermute | solution.py:360
  14.6 5.9 %collective-permute-start.5 = (bf16[896,128]{1,0:T(8,128)(2,1)S(1)}, bf16[896,128]{1,0:T(8,128)(2,1)S(1)}, u32[]{:S(2)}, u32[]{:S(2)}) collective-permute-start(bf16[896,128]{1,0:T(8,128)(2,1)S(1)} %pad_maximum_fusion.3), channel_id=1, source_target_pairs={{0,8},{8,0},{16,24},{24,16},{32,40},{40,32},{48,56},{56,48},{64,72... | collective-permute-start | bytes 688136 | tf_op jit(solution)/shard_map/ppermute | solution.py:360
  14.7 12.1 %collective-permute-start.2 = (f32[1,32,512]{2,1,0:T(8,128)S(1)}, f32[1,32,512]{2,1,0:T(8,128)S(1)}, u32[]{:S(2)}, u32[]{:S(2)}) collective-permute-start(f32[1,32,512]{2,1,0:T(8,128)S(1)} %join.1), channel_id=1, source_target_pairs={{0,4},{1,5},{2,6},{3,7},{4,0},{5,1},{6,2},{7,3},{8,12},{9,13},{10,... | collective-permute-start | bytes 196616 | tf_op jit(solution)/shard_map/ppermute | solution.py:360
  26.5 1.3 %collective-permute-start.6 = (f32[1,4096]{1,0:T(1,128)S(1)}, f32[1,4096]{1,0:T(1,128)S(1)}, u32[]{:S(2)}, u32[]{:S(2)}) collective-permute-start(f32[1,4096]{1,0:T(1,128)S(1)} %partial_sums.1), channel_id=1, source_target_pairs={{0,8},{8,0},{16,24},{24,16},{32,40},{40,32},{48,56},{56,48},{64,72... | collective-permute-start | bytes 49160 | tf_op jit(solution)/shard_map/ppermute | solution.py:360
  27.8 9.4 %collective-permute-start.7 = (f32[2,32,512]{2,1,0:T(8,128)S(1)}, f32[2,32,512]{2,1,0:T(8,128)S(1)}, u32[]{:S(2)}, u32[]{:S(2)}) collective-permute-start(f32[2,32,512]{2,1,0:T(8,128)S(1)} %pad_maximum_fusion.5), channel_id=1, source_target_pairs={{0,1},{1,0},{2,3},{3,2},{4,5},{5,4},{6,7},{7,6},{8,9},{9,8},{10,11... | collective-permute-start | bytes 393224 | tf_op jit(solution)/shard_map/ppermute | solution.py:360
  28.3 3.7 %collective-permute-start.8 = (f32[1,4096]{1,0:T(1,128)S(1)}, f32[1,4096]{1,0:T(1,128)S(1)}, u32[]{:S(2)}, u32[]{:S(2)}) collective-permute-start(f32[1,4096]{1,0:T(1,128)S(1)} %add.14), channel_id=1, source_target_pairs={{0,16},{8,24},{16,0},{24,8},{32,48},{40,56},{48,32},{56,40},{64,80... | collective-permute-start | bytes 49160 | tf_op jit(solution)/shard_map/ppermute | solution.py:360
  32.1 5.0 %collective-permute-start.9 = (f32[1,4096]{1,0:T(1,128)S(1)}, f32[1,4096]{1,0:T(1,128)S(1)}, u32[]{:S(2)}, u32[]{:S(2)}) collective-permute-start(f32[1,4096]{1,0:T(1,128)S(1)} %add.15), channel_id=1, source_target_pairs={{0,48},{8,56},{16,32},{24,40},{32,16},{40,24},{48,0},{56,8},{64,11... | collective-permute-start | bytes 49160 | tf_op jit(solution)/shard_map/ppermute | solution.py:360
  37.2 11.0 %collective-permute-start.12 = (f32[4,32,512]{2,1,0:T(8,128)S(1)}, f32[4,32,512]{2,1,0:T(8,128)S(1)}, u32[]{:S(2)}, u32[]{:S(2)}) collective-permute-start(f32[4,32,512]{2,1,0:T(8,128)S(1)} %pad_maximum_fusion.2), channel_id=1, source_target_pairs={{0,3},{1,2},{2,1},{3,0},{4,7},{5,6},{6,5},{7,4},{8,11},{9,10},{10,... | collective-permute-start | bytes 786440 | tf_op jit(solution)/shard_map/ppermute | solution.py:360
  39.7 3.7 %collective-permute-start.10 = (f32[1,4096]{1,0:T(1,128)S(1)}, f32[1,4096]{1,0:T(1,128)S(1)}, u32[]{:S(2)}, u32[]{:S(2)}) collective-permute-start(f32[1,4096]{1,0:T(1,128)S(1)} %add.16), channel_id=1, source_target_pairs={{0,64},{8,72},{16,80},{24,88},{32,96},{40,104},{48,112},{56,120},{... | collective-permute-start | bytes 49160 | tf_op jit(solution)/shard_map/ppermute | solution.py:360
  43.4 4.7 %collective-permute-start.11 = (f32[1,4096]{1,0:T(1,128)S(1)}, f32[1,4096]{1,0:T(1,128)S(1)}, u32[]{:S(2)}, u32[]{:S(2)}) collective-permute-start(f32[1,4096]{1,0:T(1,128)S(1)} %add.17.mine_ref), channel_id=1, source_target_pairs={{0,128},{8,136},{16,144},{24,152},{32,160},{40,168},{48,176},{56,1... | collective-permute-start | bytes 49160 | tf_op jit(solution)/shard_map/ppermute | solution.py:360

commit v4 on v3

--- a/solution.py
+++ b/solution.py
@@ -170,20 +170,18 @@
 
 def table_kernel(words_ref, after_ref, sign_ref):
     feat = lax.axis_index("feat")
-    first_word = ((PIECES * COLS * (feat >> 2)) * 34953) >> 20
-    words = words_ref[pl.ds(first_word, 64), :]
-    octets = jnp.concatenate(
-        [((words >> (8 * p)) & 255).astype(F32) for p in range(4)], axis=0
-    ).astype(BF16)
     for e in range(PIECES):
-        col = COLS * (feat ^ PIECE[e]) + iota((COLS, 128), 0)
+        first_col = COLS * (feat ^ PIECE[e])
+        first_word = (first_col * 34953) >> 20
+        words = words_ref[pl.ds(first_word, 32), :]
+        octets = jnp.concatenate(
+            [((words >> (8 * p)) & 255).astype(F32) for p in range(4)], axis=0
+        ).astype(BF16)
+        col = first_col + iota((COLS, 128), 0)
         word = (col * 34953) >> 20
         bit = col - 30 * word
-        target = ((bit >> 3) << 6) + (word - first_word)
-        lane = iota((COLS, 128), 1)
-        pick = jnp.concatenate(
-            [one_hot(lane == target), one_hot(lane + 128 == target)], axis=1
-        ).astype(BF16)
+        target = ((bit >> 3) << 5) + (word - first_word)
+        pick = one_hot(iota((COLS, 128), 1) == target).astype(BF16)
         octet = jnp.dot(pick, octets, preferred_element_type=F32).astype(I32)
         sign_ref[COLS * e : COLS * e + COLS, :] = sign_of((octet >> (bit & 7)) & 1)
 

time: 49 us -> 49 us (level)
  no operation moved by 1% of the time
where the time goes in v4:
time: 49 us; the launch traced here: 48.9 us
  starting transfers between devices  22.1 us (45%)
  waiting for transfers between devices  14.5 us (30%)
  Pallas kernels  9.6 us (20%)
  between operations  1.5 us (3%)
  other arithmetic  1.12 us (2%)
    ppermute x13, starting transfers between devices, swap(): return lax.ppermute(value, axis, [(i, i ^ step) for i in range(size)])  22.1 us
    ppermute x13, waiting for transfers between devices, swap(): return lax.ppermute(value, axis, [(i, i ^ step) for i in range(size)])  14.5 us
    pallas_call x1, Pallas kernels, partial_sums(): pl.pallas_call(main_kernel, out_shape=jax.ShapeDtypeStruct((1, PROJ), F32...  5.97 us
    pallas_call x1, Pallas kernels, sort_coords(): pl.pallas_call(sort_kernel, out_shape=(jax.ShapeDtypeStruct((3 * MAXB, BL...  1.55 us
  transfers between devices with their start and end apart: 13, of which 6 were waited for; matrix products, arithmetic and copies ran while one was open for 2% of the time, Pallas kernels for 18%

profile of v4, /device:TPU:8, one launch (start us, length us, event | category | flops | bytes accessed | tf_op | source)
XLA Modules:
  0.0 48.9 jit_solution(18106804211617162438)
XLA Ops:
  0.6 3.4 %collective-permute-start = (bf16[1,128,128]{2,1,0:T(8,128)(2,1)}, bf16[1,128,128]{2,1,0:T(8,128)(2,1)S(1)}, u32[]{:S(2)}, u32[]{:S(2)}) collective-permute-start(bf16[1,128,128]{2,1,0:T(8,128)(2,1)} %param.7), channel_id=1, source_target_pairs={{0,128},{8,136},{16,144},{24,152},{32,160},{40,168},{48,176},{56,1... | collective-permute-start | bytes 98312 | tf_op jit(solution)/shard_map/ppermute | solution.py:358
  4.0 1.5 %collective-permute-start.4 = (bf16[448,128]{1,0:T(8,128)(2,1)}, bf16[448,128]{1,0:T(8,128)(2,1)S(1)}, u32[]{:S(2)}, u32[]{:S(2)}) collective-permute-start(bf16[448,128]{1,0:T(8,128)(2,1)} %bitcast.14), channel_id=1, source_target_pairs={{0,16},{8,24},{16,0},{24,8},{32,48},{40,56},{48,32},{56,40},{64,80... | collective-permute-start | bytes 344072 | tf_op jit(solution)/shard_map/ppermute | solution.py:358
  6.1 0.0 copy-start.2
  6.1 0.0 copy-start.3
  6.2 0.9 %pad_maximum_fusion.4.after_ref = bf16[576,128]{1,0:T(8,128)(2,1)S(1)} fusion(bf16[448,128]{1,0:T(8,128)(2,1)} %bitcast.15, bf16[128,128]{1,0:T(8,128)(2,1)} %bitcast.16), kind=kLoop, calls=%fused_computation.4 | loop fusion | flops 294912 | bytes 294912 | tf_op jit(solution)/shard_map/concatenate | solution.py:365
  7.1 0.0 copy-done.2
  7.1 0.0 copy-done.3
  7.1 0.0 copy-start
  7.1 0.8 %rank_coords.1 = (s32[32,128]{1,0:T(8,128)S(1)}, s32[8,128]{1,0:T(8,128)S(1)}) custom-call(s32[40,128]{1,0:T(8,128)S(1)} %pad_bitcast_fusion.ints_ref.coord_ref, bf16[576,128]{1,0:T(8,128)(2,1)S(1)} %pad_maximum_fusion.4.after_ref), custom_call_target="tpu_custom_call" | custom-call | flops 1000000000 | bytes 1000000 | tf_op jit(solution)/shard_map/rank_coords/pallas_call | solution.py:102
  7.9 0.0 collective-permute-done
  8.0 2.0 %collective-permute-start.1 = (bf16[2,128,128]{2,1,0:T(8,128)(2,1)S(1)}, bf16[2,128,128]{2,1,0:T(8,128)(2,1)S(1)}, u32[]{:S(2)}, u32[]{:S(2)}) collective-permute-start(bf16[2,128,128]{2,1,0:T(8,128)(2,1)S(1)} %pad_maximum_fusion.6.after_ref), channel_id=1, source_target_pairs={{0,64},{8,72},{16,80},{24,88},{32,96},{40,104},{48,112},{56,120},{... | collective-permute-start | bytes 196616 | tf_op jit(solution)/shard_map/ppermute | solution.py:358
  10.0 0.0 copy-done
  10.0 0.6 %sign_table.1.after_too_ref.sign_ref = f32[1792,128]{1,0:T(8,128)S(1)} custom-call(s32[547,128]{1,0:T(8,128)S(1)} %bitcast.12, bf16[2,128,128]{2,1,0:T(8,128)(2,1)S(1)} %pad_maximum_fusion.6.after_ref), custom_call_target="tpu_custom_call" | custom-call | flops 2000000000 | bytes 1000000 | tf_op jit(solution)/shard_map/sign_table/pallas_call | solution.py:190
  10.6 1.5 %sort_coords.1 = (s32[288,128]{1,0:T(8,128)S(1)}, bf16[128,4096]{1,0:T(8,128)(2,1)S(1)}, bf16[96,4096]{1,0:T(8,128)(2,1)S(1)}) custom-call(s32[40,128]{1,0:T(8,128)S(1)} %pad_bitcast_fusion.ints_ref.coord_ref, s32[32,128]{1,0:T(8,128)S(1)} %get-tuple-element.19.place_ref, bf16[2,128,128]{2,1,0:T(8,128)(2,1)S(1)} %pad_maximum_fusion.6.after_ref, ...), custom_call_target="tpu_custom_call" | custom-call | flops 2000000000 | bytes 1000000 | tf_op jit(solution)/shard_map/sort_coords/pallas_call | solution.py:138
  12.1 0.2 collective-permute-done.1
  12.3 0.0 copy-start.1
  12.3 2.2 %collective-permute-start.3 = (bf16[4,128,128]{2,1,0:T(8,128)(2,1)S(1)}, bf16[4,128,128]{2,1,0:T(8,128)(2,1)S(1)}, u32[]{:S(2)}, u32[]{:S(2)}) collective-permute-start(bf16[4,128,128]{2,1,0:T(8,128)(2,1)S(1)} %constant_dynamic-update-slice_fusion.refs_1_), channel_id=1, source_target_pairs={{0,48},{8,56},{16,32},{24,40},{32,16},{40,24},{48,0},{56,8},{64,11... | collective-permute-start | bytes 393224 | tf_op jit(solution)/shard_map/ppermute | solution.py:358
  14.5 0.0 collective-permute-done.4
  14.6 0.1 collective-permute-start.5
  14.7 0.0 copy-done.1
  14.7 5.7 %collective-permute-start.2 = (f32[1,32,512]{2,1,0:T(8,128)S(1)}, f32[1,32,512]{2,1,0:T(8,128)S(1)}, u32[]{:S(2)}, u32[]{:S(2)}) collective-permute-start(f32[1,32,512]{2,1,0:T(8,128)S(1)} %join.1), channel_id=1, source_target_pairs={{0,4},{1,5},{2,6},{3,7},{4,0},{5,1},{6,2},{7,3},{8,12},{9,13},{10,... | collective-permute-start | bytes 196616 | tf_op jit(solution)/shard_map/ppermute | solution.py:358
  20.4 0.0 collective-permute-done.3
  20.5 0.0 collective-permute-done.5
  20.5 6.0 %partial_sums.1 = f32[1,4096]{1,0:T(1,128)S(1)} custom-call(s32[8,128]{1,0:T(8,128)S(1)} %get-tuple-element.25.info_ref, s32[8,128]{1,0:T(8,128)S(1)} %slice.10.counts_ref, bf16[8,128,128]{2,1,0:T(8,128)(2,1)S(1)} %pad_maximum_fusion.1.a_ref, bf16[1792,128]{1,0:T(8,128)(2,1)S(1)} %pad_maximum_fusion.g_ref, f32[1792,128]{1,0:T(8,128)S(1)} %sign_table.1.after_too_ref.sign_ref, ...), custom_call_target="tpu_custom_call" | custom-call | flops 7000000000 | bytes 1000000 | tf_op jit(solution)/shard_map/partial_sums/pallas_call | solution.py:283
  26.5 0.3 collective-permute-start.6
  26.8 0.0 collective-permute-done.2.q1_ref
  26.8 1.0 %collective-permute-done.6 = f32[1,4096]{1,0:T(1,128)S(1)} collective-permute-done((f32[1,4096]{1,0:T(1,128)S(1)}, f32[1,4096]{1,0:T(1,128)S(1)}, u32[]{:S(2)}, u32[]{:S(2)}) %collective-permute-start.6) | collective-permute-done | bytes 16416 | tf_op jit(solution)/shard_map/ppermute | solution.py:358
  27.8 0.5 %collective-permute-start.7 = (f32[2,32,512]{2,1,0:T(8,128)S(1)}, f32[2,32,512]{2,1,0:T(8,128)S(1)}, u32[]{:S(2)}, u32[]{:S(2)}) collective-permute-start(f32[2,32,512]{2,1,0:T(8,128)S(1)} %pad_maximum_fusion.5), channel_id=1, source_target_pairs={{0,1},{1,0},{2,3},{3,2},{4,5},{5,4},{6,7},{7,6},{8,9},{9,8},{10,11... | collective-permute-start | bytes 393224 | tf_op jit(solution)/shard_map/ppermute | solution.py:358
  28.3 0.3 collective-permute-start.8
  28.7 3.4 %collective-permute-done.8 = f32[1,4096]{1,0:T(1,128)S(1)} collective-permute-done((f32[1,4096]{1,0:T(1,128)S(1)}, f32[1,4096]{1,0:T(1,128)S(1)}, u32[]{:S(2)}, u32[]{:S(2)}) %collective-permute-start.8) | collective-permute-done | bytes 16416 | tf_op jit(solution)/shard_map/ppermute | solution.py:358
  32.1 1.0 %collective-permute-start.9 = (f32[1,4096]{1,0:T(1,128)S(1)}, f32[1,4096]{1,0:T(1,128)S(1)}, u32[]{:S(2)}, u32[]{:S(2)}) collective-permute-start(f32[1,4096]{1,0:T(1,128)S(1)} %add.15), channel_id=1, source_target_pairs={{0,48},{8,56},{16,32},{24,40},{32,16},{40,24},{48,0},{56,8},{64,11... | collective-permute-start | bytes 49160 | tf_op jit(solution)/shard_map/ppermute | solution.py:358
  33.0 4.1 %collective-permute-done.9 = f32[1,4096]{1,0:T(1,128)S(1)} collective-permute-done((f32[1,4096]{1,0:T(1,128)S(1)}, f32[1,4096]{1,0:T(1,128)S(1)}, u32[]{:S(2)}, u32[]{:S(2)}) %collective-permute-start.9) | collective-permute-done | bytes 16416 | tf_op jit(solution)/shard_map/ppermute | solution.py:358
  37.1 0.0 collective-permute-done.7.q2_ref
  37.2 2.5 %collective-permute-start.12 = (f32[4,32,512]{2,1,0:T(8,128)S(1)}, f32[4,32,512]{2,1,0:T(8,128)S(1)}, u32[]{:S(2)}, u32[]{:S(2)}) collective-permute-start(f32[4,32,512]{2,1,0:T(8,128)S(1)} %pad_maximum_fusion.2), channel_id=1, source_target_pairs={{0,3},{1,2},{2,1},{3,0},{4,7},{5,6},{6,5},{7,4},{8,11},{9,10},{10,... | collective-permute-start | bytes 786440 | tf_op jit(solution)/shard_map/ppermute | solution.py:358
  39.7 1.0 %collective-permute-start.10 = (f32[1,4096]{1,0:T(1,128)S(1)}, f32[1,4096]{1,0:T(1,128)S(1)}, u32[]{:S(2)}, u32[]{:S(2)}) collective-permute-start(f32[1,4096]{1,0:T(1,128)S(1)} %add.16), channel_id=1, source_target_pairs={{0,64},{8,72},{16,80},{24,88},{32,96},{40,104},{48,112},{56,120},{... | collective-permute-start | bytes 49160 | tf_op jit(solution)/shard_map/ppermute | solution.py:358
  40.7 2.7 %collective-permute-done.10 = f32[1,4096]{1,0:T(1,128)S(1)} collective-permute-done((f32[1,4096]{1,0:T(1,128)S(1)}, f32[1,4096]{1,0:T(1,128)S(1)}, u32[]{:S(2)}, u32[]{:S(2)}) %collective-permute-start.10) | collective-permute-done | bytes 16416 | tf_op jit(solution)/shard_map/ppermute | solution.py:358
  43.4 1.6 %collective-permute-start.11 = (f32[1,4096]{1,0:T(1,128)S(1)}, f32[1,4096]{1,0:T(1,128)S(1)}, u32[]{:S(2)}, u32[]{:S(2)}) collective-permute-start(f32[1,4096]{1,0:T(1,128)S(1)} %add.17.mine_ref), channel_id=1, source_target_pairs={{0,128},{8,136},{16,144},{24,152},{32,160},{40,168},{48,176},{56,1... | collective-permute-start | bytes 49160 | tf_op jit(solution)/shard_map/ppermute | solution.py:358
  45.0 3.2 %collective-permute-done.11.other_ref = f32[1,4096]{1,0:T(1,128)S(1)} collective-permute-done((f32[1,4096]{1,0:T(1,128)S(1)}, f32[1,4096]{1,0:T(1,128)S(1)}, u32[]{:S(2)}, u32[]{:S(2)}) %collective-permute-start.11) | collective-permute-done | bytes 16416 | tf_op jit(solution)/shard_map/ppermute | solution.py:358
  48.2 0.0 collective-permute-done.12.q3_ref
  48.2 0.7 %finish.1 = (f32[1,4096]{1,0:T(1,128)}, f32[1,32]{1,0:T(1,128)}) custom-call(f32[1,4096]{1,0:T(1,128)S(1)} %add.17.mine_ref, f32[1,4096]{1,0:T(1,128)S(1)} %collective-permute-done.11.other_ref, f32[32,512]{1,0:T(8,128)S(1)} %copy-done.1, f32[1,32,512]{2,1,0:T(8,128)S(1)} %collective-permute-done.2.q1_ref, f32[2,32,512]{2,1,0:T(8,128)S(1)} %collective-permute-done.7.q2_ref, ...), custom_call_target="tpu_custom_call" | custom-call | flops 1000000000 | bytes 1000000 | tf_op jit(solution)/shard_map/finish/pallas_call | solution.py:321
  (18 shorter events, 0.2 us)
Async XLA Ops:
  0.6 7.3 %collective-permute-start = (bf16[1,128,128]{2,1,0:T(8,128)(2,1)}, bf16[1,128,128]{2,1,0:T(8,128)(2,1)S(1)}, u32[]{:S(2)}, u32[]{:S(2)}) collective-permute-start(bf16[1,128,128]{2,1,0:T(8,128)(2,1)} %param.7), channel_id=1, source_target_pairs={{0,128},{8,136},{16,144},{24,152},{32,160},{40,168},{48,176},{56,1... | collective-permute-start | bytes 98312 | tf_op jit(solution)/shard_map/ppermute | solution.py:358
  4.0 10.5 %collective-permute-start.4 = (bf16[448,128]{1,0:T(8,128)(2,1)}, bf16[448,128]{1,0:T(8,128)(2,1)S(1)}, u32[]{:S(2)}, u32[]{:S(2)}) collective-permute-start(bf16[448,128]{1,0:T(8,128)(2,1)} %bitcast.14), channel_id=1, source_target_pairs={{0,16},{8,24},{16,0},{24,8},{32,48},{40,56},{48,32},{56,40},{64,80... | collective-permute-start | bytes 344072 | tf_op jit(solution)/shard_map/ppermute | solution.py:358
  6.1 0.9 %copy-start.2 = (s32[4096]{0:T(1024)S(1)}, s32[4096]{0:T(1024)}, u32[]{:S(2)}) copy-start(s32[4096]{0:T(1024)} %param.12) | copy-start | bytes 49156
  6.1 0.9 %copy-start.3 = (s32[4096]{0:T(1024)S(1)}, s32[4096]{0:T(1024)}, u32[]{:S(2)}) copy-start(s32[4096]{0:T(1024)} %param.11) | copy-start | bytes 49156
  7.1 2.8 %copy-start = (s32[128,547]{0,1:T(8,128)S(1)}, s32[128,547]{0,1:T(8,128)}, u32[]{:S(2)}) copy-start(s32[128,547]{0,1:T(8,128)} %param.10) | copy-start | bytes 840196
  8.0 4.4 %collective-permute-start.1 = (bf16[2,128,128]{2,1,0:T(8,128)(2,1)S(1)}, bf16[2,128,128]{2,1,0:T(8,128)(2,1)S(1)}, u32[]{:S(2)}, u32[]{:S(2)}) collective-permute-start(bf16[2,128,128]{2,1,0:T(8,128)(2,1)S(1)} %pad_maximum_fusion.6.after_ref), channel_id=1, source_target_pairs={{0,64},{8,72},{16,80},{24,88},{32,96},{40,104},{48,112},{56,120},{... | collective-permute-start | bytes 196616 | tf_op jit(solution)/shard_map/ppermute | solution.py:358
  12.3 2.3 %copy-start.1 = (f32[32,512]{1,0:T(8,128)S(1)}, f32[32,512]{1,0:T(8,128)}, u32[]{:S(2)}) copy-start(f32[32,512]{1,0:T(8,128)} %q0_ref.1) | copy-start | bytes 196612
  12.3 8.1 %collective-permute-start.3 = (bf16[4,128,128]{2,1,0:T(8,128)(2,1)S(1)}, bf16[4,128,128]{2,1,0:T(8,128)(2,1)S(1)}, u32[]{:S(2)}, u32[]{:S(2)}) collective-permute-start(bf16[4,128,128]{2,1,0:T(8,128)(2,1)S(1)} %constant_dynamic-update-slice_fusion.refs_1_), channel_id=1, source_target_pairs={{0,48},{8,56},{16,32},{24,40},{32,16},{40,24},{48,0},{56,8},{64,11... | collective-permute-start | bytes 393224 | tf_op jit(solution)/shard_map/ppermute | solution.py:358
  14.6 5.9 %collective-permute-start.5 = (bf16[896,128]{1,0:T(8,128)(2,1)S(1)}, bf16[896,128]{1,0:T(8,128)(2,1)S(1)}, u32[]{:S(2)}, u32[]{:S(2)}) collective-permute-start(bf16[896,128]{1,0:T(8,128)(2,1)S(1)} %pad_maximum_fusion.3), channel_id=1, source_target_pairs={{0,8},{8,0},{16,24},{24,16},{32,40},{40,32},{48,56},{56,48},{64,72... | collective-permute-start | bytes 688136 | tf_op jit(solution)/shard_map/ppermute | solution.py:358
  14.7 12.1 %collective-permute-start.2 = (f32[1,32,512]{2,1,0:T(8,128)S(1)}, f32[1,32,512]{2,1,0:T(8,128)S(1)}, u32[]{:S(2)}, u32[]{:S(2)}) collective-permute-start(f32[1,32,512]{2,1,0:T(8,128)S(1)} %join.1), channel_id=1, source_target_pairs={{0,4},{1,5},{2,6},{3,7},{4,0},{5,1},{6,2},{7,3},{8,12},{9,13},{10,... | collective-permute-start | bytes 196616 | tf_op jit(solution)/shard_map/ppermute | solution.py:358
  26.5 1.3 %collective-permute-start.6 = (f32[1,4096]{1,0:T(1,128)S(1)}, f32[1,4096]{1,0:T(1,128)S(1)}, u32[]{:S(2)}, u32[]{:S(2)}) collective-permute-start(f32[1,4096]{1,0:T(1,128)S(1)} %partial_sums.1), channel_id=1, source_target_pairs={{0,8},{8,0},{16,24},{24,16},{32,40},{40,32},{48,56},{56,48},{64,72... | collective-permute-start | bytes 49160 | tf_op jit(solution)/shard_map/ppermute | solution.py:358
  27.8 9.4 %collective-permute-start.7 = (f32[2,32,512]{2,1,0:T(8,128)S(1)}, f32[2,32,512]{2,1,0:T(8,128)S(1)}, u32[]{:S(2)}, u32[]{:S(2)}) collective-permute-start(f32[2,32,512]{2,1,0:T(8,128)S(1)} %pad_maximum_fusion.5), channel_id=1, source_target_pairs={{0,1},{1,0},{2,3},{3,2},{4,5},{5,4},{6,7},{7,6},{8,9},{9,8},{10,11... | collective-permute-start | bytes 393224 | tf_op jit(solution)/shard_map/ppermute | solution.py:358
  28.3 3.7 %collective-permute-start.8 = (f32[1,4096]{1,0:T(1,128)S(1)}, f32[1,4096]{1,0:T(1,128)S(1)}, u32[]{:S(2)}, u32[]{:S(2)}) collective-permute-start(f32[1,4096]{1,0:T(1,128)S(1)} %add.14), channel_id=1, source_target_pairs={{0,16},{8,24},{16,0},{24,8},{32,48},{40,56},{48,32},{56,40},{64,80... | collective-permute-start | bytes 49160 | tf_op jit(solution)/shard_map/ppermute | solution.py:358
  32.1 5.0 %collective-permute-start.9 = (f32[1,4096]{1,0:T(1,128)S(1)}, f32[1,4096]{1,0:T(1,128)S(1)}, u32[]{:S(2)}, u32[]{:S(2)}) collective-permute-start(f32[1,4096]{1,0:T(1,128)S(1)} %add.15), channel_id=1, source_target_pairs={{0,48},{8,56},{16,32},{24,40},{32,16},{40,24},{48,0},{56,8},{64,11... | collective-permute-start | bytes 49160 | tf_op jit(solution)/shard_map/ppermute | solution.py:358
  37.2 11.0 %collective-permute-start.12 = (f32[4,32,512]{2,1,0:T(8,128)S(1)}, f32[4,32,512]{2,1,0:T(8,128)S(1)}, u32[]{:S(2)}, u32[]{:S(2)}) collective-permute-start(f32[4,32,512]{2,1,0:T(8,128)S(1)} %pad_maximum_fusion.2), channel_id=1, source_target_pairs={{0,3},{1,2},{2,1},{3,0},{4,7},{5,6},{6,5},{7,4},{8,11},{9,10},{10,... | collective-permute-start | bytes 786440 | tf_op jit(solution)/shard_map/ppermute | solution.py:358
  39.7 3.7 %collective-permute-start.10 = (f32[1,4096]{1,0:T(1,128)S(1)}, f32[1,4096]{1,0:T(1,128)S(1)}, u32[]{:S(2)}, u32[]{:S(2)}) collective-permute-start(f32[1,4096]{1,0:T(1,128)S(1)} %add.16), channel_id=1, source_target_pairs={{0,64},{8,72},{16,80},{24,88},{32,96},{40,104},{48,112},{56,120},{... | collective-permute-start | bytes 49160 | tf_op jit(solution)/shard_map/ppermute | solution.py:358
  43.4 4.7 %collective-permute-start.11 = (f32[1,4096]{1,0:T(1,128)S(1)}, f32[1,4096]{1,0:T(1,128)S(1)}, u32[]{:S(2)}, u32[]{:S(2)}) collective-permute-start(f32[1,4096]{1,0:T(1,128)S(1)} %add.17.mine_ref), channel_id=1, source_target_pairs={{0,128},{8,136},{16,144},{24,152},{32,160},{40,168},{48,176},{56,1... | collective-permute-start | bytes 49160 | tf_op jit(solution)/shard_map/ppermute | solution.py:358
